TPU v7x, 128 devices: a whole 4x4x4 slice. The times are simulated.
128 devices in a mesh: dp: 32 (over y, x_lo, z), seq: 4 (over x_hi, core).
Axes of the slice: x: 4 (x_hi: 2, x_lo: 2; x = x_hi * 2 + x_lo), y: 4, z: 4, core: 2. Of those that a mesh axis runs over, the one named last changes fastest.
Arguments:
- layer_in: bfloat16 [64, 512, 1024], P('dp', 'seq'), may hold values from -6 to 6
- w_query: bfloat16 [1024, 1024], P(('dp', 'seq')), may hold values from -0.1875 to 0.1875
- w_key: bfloat16 [1024, 1024], P(('dp', 'seq')), may hold values from -0.1875 to 0.1875
- w_value: bfloat16 [1024, 1024], P(('dp', 'seq')), may hold values from -0.1875 to 0.1875
- w_out: bfloat16 [1024, 1024], P(('dp', 'seq')), may hold values from -1.5 to 1.5
- norm_attn: bfloat16 [1024], P(('dp', 'seq')), may hold values from 0.5 to 1.5
- norm_moe: bfloat16 [1024], P(('dp', 'seq')), may hold values from 0.5 to 1.5
- rel_table: bfloat16 [512], P(('dp', 'seq')), may hold values from -4 to 4
- w_router: bfloat16 [1024, 32], P(('dp', 'seq')), may hold values from -0.125 to 0.125
- expert_gate: bfloat16 [32, 1024, 2816], P('dp', None, 'seq'), may hold values from -0.1875 to 0.1875
- expert_up: bfloat16 [32, 1024, 2816], P('dp', None, 'seq'), may hold values from -0.1875 to 0.1875
- expert_down: bfloat16 [32, 2816, 1024], P('dp', 'seq'), may hold values from -0.109375 to 0.109375
- routes: int32 [64, 512, 2], P('dp', 'seq'), may hold values from 0 to 31, all different within a row; in each aligned block of 128 rows (0 to 127, 128 to 255, ..., all dimensions but the last counted through in order) at most 16 rows name the same one
- rel_bucket: int32 [1023], replicated, may hold values from 0 to 31, as said below
- cotangent: bfloat16 [64, 512, 1024], P('dp', 'seq'), may hold values from -6 to 6
Outputs:
- layer_out: bfloat16 [64, 512, 1024], P('dp', 'seq')
- grad_in: float32 [64, 512, 1024], P('dp', 'seq')
- grad_query: float32 [1024, 1024], P(('dp', 'seq'))
- grad_key: float32 [1024, 1024], P(('dp', 'seq'))
- grad_value: float32 [1024, 1024], P(('dp', 'seq'))
- grad_out: float32 [1024, 1024], P(('dp', 'seq'))
- grad_norm_attn: float32 [1024], P(('dp', 'seq'))
- grad_norm_moe: float32 [1024], P(('dp', 'seq'))
- grad_rel_table: float32 [512], P(('dp', 'seq'))
- grad_router: float32 [1024, 32], P(('dp', 'seq'))
- grad_gate: float32 [32, 1024, 2816], P('dp', None, 'seq')
- grad_up: float32 [32, 1024, 2816], P('dp', None, 'seq')
- grad_down: float32 [32, 2816, 1024], P('dp', 'seq')
- expert_counts: int32 [2, 32], replicated
Inputs may be any that keep to these rules, and one draw needn't show every extreme that they name: `routes`: in each aligned block of 128 rows (one item's positions on one device) no expert is named by more than 16 rows; the two entries of a row differ. `rel_bucket`: 0 at offset 0; for offsets d >= 0 below 16 and for d < 0 at or above it; does not fall as |d| grows on either side.
All inputs are finite; a program needn't handle non-finite values.
Results may differ from a plain program's by a relative error of at most 0.025.
Values may be sent and summed in bfloat16 or wider, within the bound.
A program may use at most 256 MiB of HBM per device.

v0:
```python
import jax
import jax.numpy as jnp
from jax import lax
from jax.sharding import PartitionSpec as P

HEADS = 16
BUCKETS = 32


EPSILON = 1e-06


def rms_forward(values, gain):
    factor = lax.rsqrt(jnp.mean(values * values, -1, keepdims=True) + EPSILON)
    normed = values * factor
    return (normed, factor, normed * gain)


def rms_backward(grad_output, normed, factor, gain):
    grad_gain = jnp.sum(grad_output * normed, 0)
    grad_normed = grad_output * gain
    grad_values = factor * (
        grad_normed - normed * jnp.mean(grad_normed * normed, -1, keepdims=True)
    )
    return (grad_values, grad_gain)


def gelu_grad(preact, grad_output):
    return jax.vjp(jax.nn.gelu, preact)[1](grad_output)[0]


def to_experts(buffer, dp_count, exp_count, capacity, model_width):
    shaped = buffer.reshape(dp_count, exp_count, capacity, model_width).transpose(1, 0, 2, 3)
    return shaped.reshape(exp_count, dp_count * capacity, model_width)


def from_experts(buffer, dp_count, exp_count, capacity, model_width):
    shaped = buffer.reshape(exp_count, dp_count, capacity, model_width).transpose(1, 0, 2, 3)
    return shaped.reshape(dp_count, exp_count * capacity, model_width)


def body(
    layer_in,
    w_query,
    w_key,
    w_value,
    w_out,
    norm_attn,
    norm_moe,
    rel_table,
    w_router,
    expert_gate,
    expert_up,
    expert_down,
    routes,
    rel_bucket,
    cotangent,
):
    item_count, row_count, model_width = layer_in.shape
    token_count = item_count * row_count
    length = (rel_bucket.shape[0] + 1) // 2
    head_count = HEADS
    head_size = model_width // head_count
    bucket_count = BUCKETS
    scale = head_size ** (-0.5)
    gathered = (
        lax.all_gather(w_query, ("dp", "seq"), axis=0, tiled=True),
        lax.all_gather(w_key, ("dp", "seq"), axis=0, tiled=True),
        lax.all_gather(w_value, ("dp", "seq"), axis=0, tiled=True),
        lax.all_gather(w_out, ("dp", "seq"), axis=0, tiled=True),
        lax.all_gather(w_router, ("dp", "seq"), axis=0, tiled=True),
        lax.all_gather(norm_attn, ("dp", "seq"), axis=0, tiled=True),
        lax.all_gather(norm_moe, ("dp", "seq"), axis=0, tiled=True),
        lax.all_gather(rel_table, ("dp", "seq"), axis=0, tiled=True),
    )
    full_query, full_key, full_value, full_out, full_router, gain_attn, gain_moe, table_flat = (
        gathered
    )
    gain_attn = gain_attn.astype(jnp.float32)
    gain_moe = gain_moe.astype(jnp.float32)
    table = table_flat.astype(jnp.float32).reshape(bucket_count, head_count)
    inputs = layer_in.astype(jnp.float32).reshape(token_count, model_width)
    normed_one, factor_one, hidden_one = rms_forward(inputs, gain_attn)
    hidden_one = hidden_one.astype(jnp.bfloat16)
    query = jnp.dot(hidden_one, full_query, preferred_element_type=jnp.float32).astype(jnp.bfloat16)
    key_local = jnp.dot(hidden_one, full_key, preferred_element_type=jnp.float32).astype(
        jnp.bfloat16
    )
    value_local = jnp.dot(hidden_one, full_value, preferred_element_type=jnp.float32).astype(
        jnp.bfloat16
    )
    key_all, value_all = (
        lax.all_gather(
            key_local.reshape(item_count, row_count, model_width), "seq", axis=1, tiled=True
        ),
        lax.all_gather(
            value_local.reshape(item_count, row_count, model_width), "seq", axis=1, tiled=True
        ),
    )
    query_heads = query.reshape(item_count, row_count, head_count, head_size)
    key_heads = key_all.reshape(item_count, length, head_count, head_size)
    value_heads = value_all.reshape(item_count, length, head_count, head_size)
    first_row = lax.axis_index("seq") * row_count
    offsets = (
        jnp.arange(length, dtype=jnp.int32)[None, :]
        - (first_row + jnp.arange(row_count, dtype=jnp.int32))[:, None]
        + (length - 1)
    )
    buckets = jnp.take(rel_bucket, offsets)
    bucket_hot = (
        buckets[:, :, None] == jnp.arange(bucket_count, dtype=jnp.int32)[None, None, :]
    ).astype(jnp.float32)
    position_bias = jnp.einsum("qkb,bh->hqk", bucket_hot, table, precision=lax.Precision.HIGHEST)

    def score_rows():
        raw = jnp.einsum(
            "iqhd,ikhd->ihqk", query_heads, key_heads, preferred_element_type=jnp.float32
        )
        return raw * scale + position_bias[None]

    scores = score_rows()
    top_score = jnp.max(scores, -1, keepdims=True)
    log_total = top_score + jnp.log(jnp.sum(jnp.exp(scores - top_score), -1, keepdims=True))
    probs_low = jnp.exp(scores - log_total).astype(jnp.bfloat16)
    mixed = jnp.einsum(
        "ihqk,ikhd->iqhd", probs_low, value_heads, preferred_element_type=jnp.float32
    )
    mixed = mixed.astype(jnp.bfloat16).reshape(token_count, model_width)
    resid = inputs + jnp.dot(mixed, full_out, preferred_element_type=jnp.float32)
    normed_two, factor_two, hidden_two = rms_forward(resid, gain_moe)
    hidden_two = hidden_two.astype(jnp.bfloat16)
    logits = jnp.dot(hidden_two, full_router, preferred_element_type=jnp.float32)
    experts = full_router.shape[1]
    route_flat = routes.reshape(token_count, 2)
    choose_hot = route_flat[:, :, None] == jnp.arange(experts, dtype=jnp.int32)[None, None, :]
    chosen = jnp.sum(jnp.where(choose_hot, logits[:, None, :], 0.0), -1)
    gates = jax.nn.softmax(chosen, -1)
    order_hot = choose_hot.transpose(1, 0, 2).reshape(2 * token_count, experts).astype(jnp.int32)
    earlier = jnp.cumsum(order_hot, 0) - order_hot
    slot_order = jnp.sum(earlier * order_hot, -1)
    capacity = max(2, (10 * token_count + 4 * experts - 1) // (4 * experts))
    dropped = jnp.sum(order_hot * (slot_order >= capacity)[:, None].astype(jnp.int32), 0)
    tallies = jnp.stack([jnp.sum(order_hot, 0), dropped])
    totals = lax.psum(tallies, ("dp", "seq"))
    slots = slot_order.reshape(2, token_count).transpose(1, 0)
    target = jnp.where(slots < capacity, route_flat * capacity + slots, -1)
    slot_hot = (
        target[:, :, None] == jnp.arange(experts * capacity, dtype=jnp.int32)[None, None, :]
    ).astype(jnp.bfloat16)
    dp_count = lax.axis_size("dp")
    exp_count = expert_gate.shape[0]
    outgoing = jnp.einsum(
        "tkc,td->cd", slot_hot, hidden_two, preferred_element_type=jnp.float32
    ).astype(jnp.bfloat16)
    incoming = lax.all_to_all(
        outgoing.reshape(dp_count, exp_count * capacity, model_width),
        "dp",
        split_axis=0,
        concat_axis=0,
        tiled=True,
    )
    expert_rows = to_experts(incoming, dp_count, exp_count, capacity, model_width)
    gate_full, up_full, down_full = (
        lax.all_gather(expert_gate, "seq", axis=2, tiled=True),
        lax.all_gather(expert_up, "seq", axis=2, tiled=True),
        lax.all_gather(expert_down, "seq", axis=1, tiled=True),
    )
    gate_pre = jnp.einsum(
        "erd,edf->erf", expert_rows, gate_full, preferred_element_type=jnp.float32
    )
    up_pre = jnp.einsum("erd,edf->erf", expert_rows, up_full, preferred_element_type=jnp.float32)
    gate_value = jax.nn.gelu(gate_pre)
    active = (gate_value * up_pre).astype(jnp.bfloat16)
    expert_out = jnp.einsum(
        "erf,efd->erd", active, down_full, preferred_element_type=jnp.float32
    ).astype(jnp.bfloat16)
    returning = from_experts(expert_out, dp_count, exp_count, capacity, model_width)
    results = lax.all_to_all(returning, "dp", split_axis=0, concat_axis=0, tiled=True).reshape(
        experts * capacity, model_width
    )
    picked = jnp.einsum("tkc,cd->tkd", slot_hot, results, preferred_element_type=jnp.float32)
    moe_out = jnp.sum(gates[:, :, None] * picked, 1)
    layer_out = (resid + moe_out).astype(jnp.bfloat16).reshape(item_count, row_count, model_width)
    grad_final = cotangent.astype(jnp.float32).reshape(token_count, model_width)
    grad_gates = jnp.sum(grad_final[:, None, :] * picked, -1)
    grad_sent = (gates[:, :, None] * grad_final[:, None, :]).astype(jnp.bfloat16)
    grad_slots = jnp.einsum(
        "tkc,tkd->cd", slot_hot, grad_sent, preferred_element_type=jnp.float32
    ).astype(jnp.bfloat16)
    grad_arrived = lax.all_to_all(
        grad_slots.reshape(dp_count, exp_count * capacity, model_width),
        "dp",
        split_axis=0,
        concat_axis=0,
        tiled=True,
    )
    grad_expert = to_experts(grad_arrived, dp_count, exp_count, capacity, model_width)
    grad_active = jnp.einsum(
        "erd,efd->erf", grad_expert, down_full, preferred_element_type=jnp.float32
    )
    grad_down_full = jnp.einsum(
        "erf,erd->efd", active, grad_expert, preferred_element_type=jnp.float32
    )
    grad_gate_pre = gelu_grad(gate_pre, grad_active * up_pre).astype(jnp.bfloat16)
    grad_up_pre = (grad_active * gate_value).astype(jnp.bfloat16)
    grad_gate_full = jnp.einsum(
        "erd,erf->edf", expert_rows, grad_gate_pre, preferred_element_type=jnp.float32
    )
    grad_up_full = jnp.einsum(
        "erd,erf->edf", expert_rows, grad_up_pre, preferred_element_type=jnp.float32
    )
    grad_rows = jnp.einsum(
        "erf,edf->erd", grad_gate_pre, gate_full, preferred_element_type=jnp.float32
    )
    grad_rows = (
        grad_rows
        + jnp.einsum("erf,edf->erd", grad_up_pre, up_full, preferred_element_type=jnp.float32)
    ).astype(jnp.bfloat16)
    grad_gate, grad_up, grad_down = (
        lax.psum_scatter(
            grad_gate_full.astype(jnp.bfloat16), "seq", scatter_dimension=2, tiled=True
        ).astype(jnp.float32),
        lax.psum_scatter(
            grad_up_full.astype(jnp.bfloat16), "seq", scatter_dimension=2, tiled=True
        ).astype(jnp.float32),
        lax.psum_scatter(
            grad_down_full.astype(jnp.bfloat16), "seq", scatter_dimension=1, tiled=True
        ).astype(jnp.float32),
    )
    grad_leaving = from_experts(grad_rows, dp_count, exp_count, capacity, model_width)
    grad_slot_rows = lax.all_to_all(
        grad_leaving, "dp", split_axis=0, concat_axis=0, tiled=True
    ).reshape(experts * capacity, model_width)
    grad_from_experts = jnp.einsum(
        "tkc,cd->td", slot_hot, grad_slot_rows, preferred_element_type=jnp.float32
    )
    grad_chosen = gates * (grad_gates - jnp.sum(gates * grad_gates, -1, keepdims=True))
    grad_logits = jnp.sum(jnp.where(choose_hot, grad_chosen[:, :, None], 0.0), 1).astype(
        jnp.bfloat16
    )
    grad_router_part = jnp.dot(hidden_two.T, grad_logits, preferred_element_type=jnp.float32)
    grad_hidden_two = grad_from_experts + jnp.dot(
        grad_logits, full_router.T, preferred_element_type=jnp.float32
    )
    grad_resid_norm, grad_gain_moe = rms_backward(grad_hidden_two, normed_two, factor_two, gain_moe)
    grad_resid = grad_final + grad_resid_norm
    grad_attended = grad_resid.astype(jnp.bfloat16)
    grad_out_part = jnp.dot(mixed.T, grad_attended, preferred_element_type=jnp.float32)
    grad_mixed = jnp.dot(grad_attended, full_out.T, preferred_element_type=jnp.float32).astype(
        jnp.bfloat16
    )
    grad_mixed = grad_mixed.reshape(item_count, row_count, head_count, head_size)
    probs_again = jnp.exp(score_rows() - log_total)
    grad_probs = jnp.einsum(
        "iqhd,ikhd->ihqk", grad_mixed, value_heads, preferred_element_type=jnp.float32
    )
    grad_value_all = jnp.einsum(
        "ihqk,iqhd->ikhd",
        probs_again.astype(jnp.bfloat16),
        grad_mixed,
        preferred_element_type=jnp.float32,
    )
    grad_scores = (
        probs_again * (grad_probs - jnp.sum(probs_again * grad_probs, -1, keepdims=True))
    ).astype(jnp.bfloat16)
    grad_query_heads = (
        jnp.einsum("ihqk,ikhd->iqhd", grad_scores, key_heads, preferred_element_type=jnp.float32)
        * scale
    )
    grad_key_all = (
        jnp.einsum("ihqk,iqhd->ikhd", grad_scores, query_heads, preferred_element_type=jnp.float32)
        * scale
    )
    grad_bias = jnp.sum(grad_scores.astype(jnp.float32), 0)
    grad_table = jnp.einsum("qkb,hqk->bh", bucket_hot, grad_bias, precision=lax.Precision.HIGHEST)
    grad_key_own, grad_value_own = (
        lax.psum_scatter(
            grad_key_all.reshape(item_count, length, model_width).astype(jnp.bfloat16),
            "seq",
            scatter_dimension=1,
            tiled=True,
        ).astype(jnp.float32),
        lax.psum_scatter(
            grad_value_all.reshape(item_count, length, model_width).astype(jnp.bfloat16),
            "seq",
            scatter_dimension=1,
            tiled=True,
        ).astype(jnp.float32),
    )
    grad_query_low = grad_query_heads.astype(jnp.bfloat16).reshape(token_count, model_width)
    grad_key_low = grad_key_own.astype(jnp.bfloat16).reshape(token_count, model_width)
    grad_value_low = grad_value_own.astype(jnp.bfloat16).reshape(token_count, model_width)
    grad_wq = jnp.dot(hidden_one.T, grad_query_low, preferred_element_type=jnp.float32)
    grad_wk = jnp.dot(hidden_one.T, grad_key_low, preferred_element_type=jnp.float32)
    grad_wv = jnp.dot(hidden_one.T, grad_value_low, preferred_element_type=jnp.float32)
    grad_hidden_one = jnp.dot(grad_query_low, full_query.T, preferred_element_type=jnp.float32)
    grad_hidden_one = grad_hidden_one + jnp.dot(
        grad_key_low, full_key.T, preferred_element_type=jnp.float32
    )
    grad_hidden_one = grad_hidden_one + jnp.dot(
        grad_value_low, full_value.T, preferred_element_type=jnp.float32
    )
    grad_input_norm, grad_gain_attn = rms_backward(
        grad_hidden_one, normed_one, factor_one, gain_attn
    )
    grad_in = (grad_resid + grad_input_norm).reshape(item_count, row_count, model_width)
    shards = (
        lax.psum_scatter(grad_wq, ("dp", "seq"), scatter_dimension=0, tiled=True),
        lax.psum_scatter(grad_wk, ("dp", "seq"), scatter_dimension=0, tiled=True),
        lax.psum_scatter(grad_wv, ("dp", "seq"), scatter_dimension=0, tiled=True),
        lax.psum_scatter(grad_out_part, ("dp", "seq"), scatter_dimension=0, tiled=True),
        lax.psum_scatter(grad_router_part, ("dp", "seq"), scatter_dimension=0, tiled=True),
        lax.psum_scatter(grad_gain_attn, ("dp", "seq"), scatter_dimension=0, tiled=True),
        lax.psum_scatter(grad_gain_moe, ("dp", "seq"), scatter_dimension=0, tiled=True),
        lax.psum_scatter(grad_table.reshape(-1), ("dp", "seq"), scatter_dimension=0, tiled=True),
    )
    return (
        layer_out,
        grad_in,
        shards[0],
        shards[1],
        shards[2],
        shards[3],
        shards[5],
        shards[6],
        shards[7],
        shards[4],
        grad_gate,
        grad_up,
        grad_down,
        totals,
    )


def solution(mesh):
    return jax.shard_map(
        body,
        mesh=mesh,
        in_specs=(
            P("dp", "seq", None),
            P(("dp", "seq"), None),
            P(("dp", "seq"), None),
            P(("dp", "seq"), None),
            P(("dp", "seq"), None),
            P(("dp", "seq")),
            P(("dp", "seq")),
            P(("dp", "seq")),
            P(("dp", "seq"), None),
            P("dp", None, "seq"),
            P("dp", None, "seq"),
            P("dp", "seq", None),
            P("dp", "seq", None),
            P(),
            P("dp", "seq", None),
        ),
        out_specs=(
            P("dp", "seq", None),
            P("dp", "seq", None),
            P(("dp", "seq"), None),
            P(("dp", "seq"), None),
            P(("dp", "seq"), None),
            P(("dp", "seq"), None),
            P(("dp", "seq")),
            P(("dp", "seq")),
            P(("dp", "seq")),
            P(("dp", "seq"), None),
            P("dp", None, "seq"),
            P("dp", None, "seq"),
            P("dp", "seq", None),
            P(),
        ),
        check_vma=False,
    )
```

profile of v0, /device:TPU:5, one launch (start us, length us, event | category | flops | bytes accessed | tf_op | source)
XLA Modules:
  0.0 4136.0 jit_solution(8378253393289884162)
XLA Ops:
  12.0 66.8 %all-reduce.8 = (bf16[1024]{0:T(1024)(128)(2,1)S(1)}, bf16[512]{0:T(512)(128)(2,1)S(1)}, bf16[1024]{0:T(1024)(128)(2,1)S(1)}) all-reduce(bf16[1024]{0:T(1024)(128)(2,1)S(1)} %dynamic-update-slice, bf16[512]{0:T(512)(128)(2,1)S(1)} %dynamic-update-slice.1, ...), channel_id=1, replica_groups=mesh['dp'=32,'seq'=4] {'dp','seq'}, use_global_device_ids=true, to_apply=%add | all-reduce | flops 2560 | bytes 10240
  82.4 122.8 %all-gather.10.cloned.1.call-done = bf16[1024,1024]{1,0:T(8,128)(2,1)} async-done(((bf16[8,1024]{1,0:T(8,128)(2,1)}), bf16[1024,1024]{1,0:T(8,128)(2,1)}) %all-gather.10.cloned.1.call-update) | async-done | bytes 2097168 | tf_op jit(solution)/shard_map/all_gather | solution.py:69
  208.5 191.3 %all-gather.16.cloned.1.call-done = bf16[1024,1024]{1,0:T(8,128)(2,1)} async-done(((bf16[8,1024]{1,0:T(8,128)(2,1)}), bf16[1024,1024]{1,0:T(8,128)(2,1)}) %all-gather.16.cloned.1.call-update) | async-done | bytes 2097168 | tf_op jit(solution)/shard_map/all_gather | solution.py:68
  406.0 260.7 %gather_fusion = s32[65536]{0:T(1024)S(1)} fusion(s32[1023]{0:T(1024)S(1)} %copy-done, s32[65536]{0:T(1024)S(1)} %broadcast_clamp_fusion), kind=kCustom, calls=%fused_computation | custom fusion | bytes 786432 | tf_op jit(solution)/shard_map/jit(_take)/gather | solution.py:109
  668.9 37.3 copy.106
  713.0 190.1 %all_gather.48 = bf16[1024,32]{1,0:T(8,128)(2,1)S(1)} all-gather(bf16[8,32]{1,0:T(8,128)(2,1)S(1)} %copy-done.39), channel_id=1, replica_groups=mesh['dp'=32,'seq'=4] {'dp','seq'}, dimensions={0}, use_global_device_ids=true | all-gather | bytes 66048 | tf_op jit(solution)/shard_map/all_gather | solution.py:71
  950.8 24.3 all-to-all-done.2
  983.1 32.0 all-to-all-done
  1018.4 9.9 fusion.8
  1028.4 9.9 fusion.14
  1038.3 16.9 fusion.6
  1056.9 7.6 fusion.23
  1079.6 7.6 add_convert_fusion
  1106.9 11.5 all-to-all-done.3
  1132.6 9.2 multiply_reduce_fusion
  1141.8 9.5 convert_reduce_fusion
  1163.3 8.8 convert_bitcast_fusion.2
  1172.0 26.5 copy.131
  1198.5 9.1 copy.168
  1207.7 8.6 convert_bitcast_fusion.1
  1216.3 26.4 copy.133
  1242.7 9.2 copy.167
  1253.2 9.1 convert_bitcast_fusion
  1282.0 69.2 %psum.7 = s32[2,32]{1,0:T(2,128)} all-reduce(s32[2,32]{1,0:T(2,128)S(1)} %pad_add_fusion), channel_id=1, replica_groups=mesh['dp'=32,'seq'=4] {'dp','seq'}, use_global_device_ids=true, to_apply=%region_36.37 | all-reduce | flops 64 | bytes 512 | tf_op jit(solution)/shard_map/psum | solution.py:144
  1365.5 23.2 all-reduce.11.cloned.1.call-done
  1394.7 71.6 %all-reduce.7 = (f32[1024]{0:T(1024)S(1)}, f32[1024]{0:T(1024)S(1)}, f32[512]{0:T(512)S(1)}) all-reduce(f32[1024]{0:T(1024)S(1)} %get-tuple-element.74, f32[1024]{0:T(1024)S(1)} %get-tuple-element.70, f32[512]{0:T(512)S(1)} %reshape.475), channel_id=8, replica_groups=mesh['dp'=32,'seq'=4] {'dp','seq'}, use_global_device_ids=true, to_apply=%region_25.26.clone | all-reduce | flops 2560 | bytes 20480
  1480.9 32.8 reduce-scatter.30.cloned.1.call-done
  1525.2 52.4 %reduce-scatter.26.cloned.1.call-done = bf16[1,704,1024]{2,1,0:T(8,128)(2,1)} async-done(((bf16[1,2816,1024]{2,1,0:T(8,128)(2,1)}), bf16[1,704,1024]{2,1,0:T(8,128)(2,1)}) %reduce-scatter.26.cloned.1.call-update) | async-done | bytes 1441808 | tf_op jit(solution)/shard_map/reduce_scatter | solution.py:226
  1581.0 630.5 %reduce-scatter.18.cloned.1.call-done = f32[8,1024]{1,0:T(8,128)} async-done(((f32[1024,1024]{1,0:T(8,128)}), f32[8,1024]{1,0:T(8,128)}) %reduce-scatter.18.cloned.1.call-update) | async-done | bytes 32784 | tf_op jit(solution)/shard_map/reduce_scatter | solution.py:308
  2211.5 639.3 %reduce-scatter.24.cloned.1.call-done = f32[8,1024]{1,0:T(8,128)} async-done(((f32[1024,1024]{1,0:T(8,128)}), f32[8,1024]{1,0:T(8,128)}) %reduce-scatter.24.cloned.1.call-update) | async-done | bytes 32784 | tf_op jit(solution)/shard_map/reduce_scatter | solution.py:311
  2850.7 639.2 %reduce-scatter.20.cloned.1.call-done = f32[8,1024]{1,0:T(8,128)} async-done(((f32[1024,1024]{1,0:T(8,128)}), f32[8,1024]{1,0:T(8,128)}) %reduce-scatter.20.cloned.1.call-update) | async-done | bytes 32784 | tf_op jit(solution)/shard_map/reduce_scatter | solution.py:309
  3489.9 639.4 %reduce-scatter.22.cloned.1.call-done = f32[8,1024]{1,0:T(8,128)} async-done(((f32[1024,1024]{1,0:T(8,128)}), f32[8,1024]{1,0:T(8,128)}) %reduce-scatter.22.cloned.1.call-update) | async-done | bytes 32784 | tf_op jit(solution)/shard_map/reduce_scatter | solution.py:310
  (248 shorter events, 218.2 us)
Async XLA Ops:
  7.2 398.8 %copy-start = (s32[1023]{0:T(1024)S(1)}, s32[1023]{0:T(1024)}, u32[]{:S(2)}) copy-start(s32[1023]{0:T(1024)} %param.28) | copy-start | bytes 12280
  7.2 198.1 %all-gather.10.cloned.1.call-start = ((), (), s32[]{:S(2)}) async-start(), calls=%async_computation.13 | async-start | bytes 2113536 | tf_op jit(solution)/shard_map/all_gather | solution.py:69
  7.9 391.9 %all-gather.16.cloned.1.call-start = ((), (), s32[]{:S(2)}) async-start(), calls=%async_computation.16 | async-start | bytes 2113536 | tf_op jit(solution)/shard_map/all_gather | solution.py:68
  8.7 896.0 %all-gather.14.cloned.1.call-start = ((), (), s32[]{:S(2)}) async-start(), calls=%async_computation.15 | async-start | bytes 2113536 | tf_op jit(solution)/shard_map/all_gather | solution.py:67
  9.4 899.5 %all-gather.12.cloned.1.call-start = ((), (), s32[]{:S(2)}) async-start(), calls=%async_computation.14 | async-start | bytes 2621440 | tf_op jit(solution)/shard_map/all_gather | solution.py:96
  208.4 704.7 %all-gather.18.cloned.1.call-start = ((), (), s32[]{:S(2)}) async-start(), calls=%async_computation.17 | async-start | bytes 2621440 | tf_op jit(solution)/shard_map/all_gather | solution.py:93
  403.0 526.8 %all-gather.20.cloned.1.call-start = ((), (), s32[]{:S(2)}) async-start(), calls=%async_computation.18 | async-start | bytes 2113536 | tf_op jit(solution)/shard_map/all_gather | solution.py:70
  403.5 614.9 %all-gather.26.cloned.1.call-start = ((), (), s32[]{:S(2)}) async-start(), calls=%async_computation.21 | async-start | bytes 7208960 | tf_op jit(solution)/shard_map/all_gather | solution.py:166
  404.3 624.1 %all-gather.24.cloned.1.call-start = ((), (), s32[]{:S(2)}) async-start(), calls=%async_computation.20 | async-start | bytes 7208960 | tf_op jit(solution)/shard_map/all_gather | solution.py:165
  405.0 633.2 %all-gather.22.cloned.1.call-start = ((), (), s32[]{:S(2)}) async-start(), calls=%async_computation.19 | async-start | bytes 7208960 | tf_op jit(solution)/shard_map/all_gather | solution.py:164
  707.4 195.7 %copy-start.31 = (s32[2,128,2]{1,2,0:T(2,128)S(1)}, s32[2,128,2]{1,2,0:T(2,128)}, u32[]{:S(2)}) copy-start(s32[2,128,2]{1,2,0:T(2,128)} %param.27) | copy-start | bytes 6148
  903.1 10.0 copy-start.32
  904.7 8.4 copy-start.34
  940.2 34.8 all-to-all-start.2
  975.0 40.1 all-to-all-start
  1067.7 24.7 all-to-all-start.1
  1092.4 26.0 all-to-all-start.3
  1098.2 175.9 %reduce-scatter.14.cloned.1.call-start = ((), (), s32[]{:S(2)}) async-start(), calls=%async_computation.22 | async-start | bytes 2621440 | tf_op jit(solution)/shard_map/reduce_scatter | solution.py:277
  1132.6 9.2 copy-start.18
  1132.6 9.2 copy-start.3
  1141.8 11.6 copy-start.17
  1156.5 121.5 %reduce-scatter.16.cloned.1.call-start = ((), (), s32[]{:S(2)}) async-start(), calls=%async_computation.23 | async-start | bytes 2621440 | tf_op jit(solution)/shard_map/reduce_scatter | solution.py:283
  1161.9 226.7 %all-reduce.11.cloned.1.call-start = ((), (), s32[]{:S(2)}) async-start(), calls=%async_computation.31 | async-start | bytes 1048576
  1163.2 306.2 %reduce-scatter.28.cloned.1.call-start = ((), (), s32[]{:S(2)}) async-start(), calls=%async_computation.29 | async-start | bytes 7208960
  1207.6 306.1 %reduce-scatter.30.cloned.1.call-start = ((), (), s32[]{:S(2)}) async-start(), calls=%async_computation.30 | async-start | bytes 7208960
  1251.9 325.8 %reduce-scatter.26.cloned.1.call-start = ((), (), s32[]{:S(2)}) async-start(), calls=%async_computation.28 | async-start | bytes 7208960 | tf_op jit(solution)/shard_map/reduce_scatter | solution.py:226
  1262.3 949.1 %reduce-scatter.18.cloned.1.call-start = ((), (), s32[]{:S(2)}) async-start(), calls=%async_computation.24 | async-start | bytes 4227072 | tf_op jit(solution)/shard_map/reduce_scatter | solution.py:308
  1271.2 1579.5 %reduce-scatter.24.cloned.1.call-start = ((), (), s32[]{:S(2)}) async-start(), calls=%async_computation.27 | async-start | bytes 4227072 | tf_op jit(solution)/shard_map/reduce_scatter | solution.py:311
  1274.0 2215.9 %reduce-scatter.20.cloned.1.call-start = ((), (), s32[]{:S(2)}) async-start(), calls=%async_computation.25 | async-start | bytes 4227072 | tf_op jit(solution)/shard_map/reduce_scatter | solution.py:309
  1278.0 2851.3 %reduce-scatter.22.cloned.1.call-start = ((), (), s32[]{:S(2)}) async-start(), calls=%async_computation.26 | async-start | bytes 4227072 | tf_op jit(solution)/shard_map/reduce_scatter | solution.py:310
  1363.1 29.5 copy-start.37
  1516.6 2612.7 %copy-start.1 = (s32[1023]{0:T(1024)S(1)}, s32[1023]{0:T(1024)}, u32[]{:S(2)}) copy-start(s32[1023]{0:T(1024)} %param.28) | copy-start | bytes 12280
  (33 other events, 96.1 us)
Sparse Core Ops, SparseCore 0:
  9.8 195.4 all-gather.9
  207.0 192.7 all-gather.15
  401.5 192.8 all-gather.13
  596.5 24.0 all-gather.11
  622.7 26.0 all-gather.17
  650.4 194.9 all-gather.19
  847.0 45.0 all-gather.25
  893.8 46.6 all-gather.23
  942.2 68.4 all-gather.21
  1156.7 39.2 reduce-scatter.13
  1199.4 37.7 reduce-scatter.15
  1241.8 146.8 all-reduce.10
  1391.5 58.7 reduce-scatter.27
  1452.8 60.9 reduce-scatter.29
  1516.4 61.1 reduce-scatter.25
  1580.5 630.9 reduce-scatter.17
  2214.4 636.3 reduce-scatter.23
  2853.5 636.3 reduce-scatter.19
  3492.9 636.3 reduce-scatter.21
where the time goes:
time: 4170 us; the launch traced here: 4140 us
  waiting for transfers between devices  3050 us (73%)
  local copies, waits for them, and re-layouts  466 us (11%)
  blocking collectives  398 us (10%)
  matrix products  162 us (4%)
    reduce_scatter x1, waiting for transfers between devices, body(): lax.psum_scatter(grad_wv, ('dp', 'seq'), scatter_dimension=0, tiled=True)  639 us
    reduce_scatter x1, waiting for transfers between devices, body(): lax.psum_scatter(grad_out_part, ('dp', 'seq'), scatter_dimension=0, tiled...  639 us
    reduce_scatter x1, waiting for transfers between devices, body(): lax.psum_scatter(grad_wk, ('dp', 'seq'), scatter_dimension=0, tiled=True)  639 us
    reduce_scatter x1, waiting for transfers between devices, body(): lax.psum_scatter(grad_wq, ('dp', 'seq'), scatter_dimension=0, tiled=True)  630 us
    gather x2, local copies, waits for them, and re-layouts, body(): buckets = jnp.take(rel_bucket, offsets)  261 us
    all_gather x1, waiting for transfers between devices, body(): lax.all_gather(w_key, ('dp', 'seq'), axis=0, tiled=True)  191 us
    all_gather x1, blocking collectives, body(): lax.all_gather(w_router, ('dp', 'seq'), axis=0, tiled=True)  190 us
    unnamed x2, blocking collectives  138 us
  transfers between devices with their start and end apart: 23, of which 13 were waited for; matrix products, arithmetic and copies ran while one was open for 14% of the time, Pallas kernels for 0%

commit v1 on v0

v1 whole, which is shorter than its diff:
```python
import math

import jax
import jax.numpy as jnp
from jax import lax
from jax.experimental import pallas as pl
from jax.experimental.pallas import tpu as pltpu
from jax.sharding import PartitionSpec as P

MESH = pl.DeviceIdType.MESH
ANY = pl.BlockSpec(memory_space=pl.ANY)
VMEM = pl.BlockSpec(memory_space=pltpu.VMEM)
DMA = pltpu.SemaphoreType.DMA
F32 = jnp.float32
BF16 = jnp.bfloat16

D = 1024
HEADS = 16
SIZE = 64
BUCKETS = 32
EXPERTS = 32
LENGTH = 512
ROWS = 128
CAP = 20
MAIN = 16
EPSILON = 1e-06

SLAB = 4 * 1024 + 256
PARTS = ((0, 1536), (1536, 1408), (2944, 1408))
ORDERS = ("xyz", "yzx", "zxy")
TAIL = 256 + 128
GRAD = 3 * 256 + 128 + 256
THIRD = GRAD // 3


def div(a, b):
    return lax.div(a, jnp.int32(b))


def rem(a, b):
    return lax.rem(a, jnp.int32(b))


def place():
    dp, seq = lax.axis_index("dp"), lax.axis_index("seq")
    x = div(seq, 2) * 2 + rem(div(dp, 4), 2)
    return x, div(dp, 8), rem(dp, 4), rem(seq, 2)


def device(x, y, z, core):
    return ((y * 2 + rem(x, 2)) * 4 + z, div(x, 2) * 2 + core)


def greet(devices):
    barrier = pltpu.get_barrier_semaphore()
    for one in devices:
        pl.semaphore_signal(barrier, inc=1, device_id=one, device_id_type=MESH)
    pl.semaphore_wait(barrier, len(devices))


def remote(src, dst, send, recv, to):
    return pltpu.make_async_remote_copy(
        src_ref=src, dst_ref=dst, send_sem=send, recv_sem=recv, device_id=to, device_id_type=MESH
    )


def params(collective, megabytes):
    return pltpu.CompilerParams(
        collective_id=collective, has_side_effects=True, vmem_limit_bytes=megabytes << 20
    )


def cost(sent, flops=0):
    return pl.CostEstimate(flops=flops, bytes_accessed=sent, transcendentals=0)


def seq_gather_start(own, full, relay, sems):
    local, send, recv = sems
    x, y, z, core = place()
    right, left = device(rem(x + 1, 4), y, z, core), device(rem(x + 3, 4), y, z, core)
    sibling = device(x, y, z, 1 - core)
    me = div(x, 2) * 2 + core
    mine = pltpu.make_async_copy(own, full.at[:, me], local)
    copies = [
        remote(own, full.at[:, me], send.at[0], recv.at[0], sibling),
        remote(own.at[0], relay.at[0], send.at[1], recv.at[1], right),
        remote(own.at[1], relay.at[1], send.at[2], recv.at[2], left),
    ]
    mine.start()
    for copy in copies[1:] + copies[:1]:
        copy.start()
    return mine, copies


def seq_gather_finish(state, full, relay, sems):
    local, send, recv = sems
    mine, copies = state
    x, y, z, core = place()
    right, left = device(rem(x + 1, 4), y, z, core), device(rem(x + 3, 4), y, z, core)
    sibling = device(x, y, z, 1 - core)
    from_left = div(rem(x + 3, 4), 2) * 2 + core
    from_right = div(rem(x + 1, 4), 2) * 2 + core
    partner = rem(div(x, 2) + 1, 2) * 2 + core
    onward = [
        remote(relay.at[0], full.at[0, from_left], send.at[3], recv.at[3], right),
        remote(relay.at[1], full.at[1, from_right], send.at[4], recv.at[4], left),
    ]
    across = [
        remote(full.at[0, partner], full.at[0, partner], send.at[5], recv.at[5], sibling),
        remote(full.at[1, partner], full.at[1, partner], send.at[6], recv.at[6], sibling),
    ]
    for item in range(2):
        copies[1 + item].wait_recv()
        onward[item].start()
    for item in range(2):
        onward[item].wait_recv()
        across[item].start()
    mine.wait()
    copies[0].wait_recv()
    for copy in across:
        copy.wait_recv()
    for copy in copies + onward + across:
        copy.wait_send()


def chips(k):
    x, y, z, core = place()
    kx, ky, kz = div(k, 16), rem(div(k, 4), 4), rem(k, 4)
    ahead = (rem(x + kx, 4), rem(y + ky, 4), rem(z + kz, 4))
    behind = (rem(x + 4 - kx, 4), rem(y + 4 - ky, 4), rem(z + 4 - kz, 4))
    return ahead, behind


def greet_chips():
    x, y, z, core = place()
    barrier = pltpu.get_barrier_semaphore()

    @pl.loop(1, 64)
    def _(k):
        ahead, _ = chips(k)
        pl.semaphore_signal(barrier, inc=1, device_id=device(*ahead, core), device_id_type=MESH)

    pl.semaphore_signal(barrier, inc=1, device_id=device(x, y, z, 1 - core), device_id_type=MESH)
    pl.semaphore_wait(barrier, 64)


def peers(k):
    x, y, z, core = place()
    kx, ky, kz = div(k, 16), rem(div(k, 4), 4), rem(k, 4)
    return device(div(x, 2) * 2 + rem(rem(x, 2) + kx, 2), rem(y + ky, 4), rem(z + kz, 4), core)


def greet_peers(others):
    barrier = pltpu.get_barrier_semaphore()

    @pl.loop(1, 32)
    def _(k):
        pl.semaphore_signal(barrier, inc=1, device_id=peers(k), device_id_type=MESH)

    for one in others:
        pl.semaphore_signal(barrier, inc=1, device_id=one, device_id_type=MESH)
    pl.semaphore_wait(barrier, 31 + len(others))


class Exchange:
    def __init__(self, slabs, rows, local, send, recv):
        self.slabs, self.rows = slabs, rows
        self.local, self.send, self.recv = local, send, recv
        self.dp = lax.axis_index("dp")

    def packet(self, k):
        to = peers(k)
        return [
            remote(slab.at[to[0]], rows.at[self.dp], self.send.at[i, k], self.recv.at[i, k], to)
            for i, (slab, rows) in enumerate(zip(self.slabs, self.rows))
        ]

    def kept(self):
        return [
            pltpu.make_async_copy(slab.at[self.dp], rows.at[self.dp], self.local.at[i])
            for i, (slab, rows) in enumerate(zip(self.slabs, self.rows))
        ]

    def start(self, first, last):
        @pl.loop(first, last)
        def _(k):
            for copy in self.packet(k):
                copy.start()

    def keep(self):
        for copy in self.kept():
            copy.start()

    def finish(self):
        @pl.loop(1, 32)
        def _(k):
            for copy in self.packet(k):
                copy.wait_recv()
                copy.wait_send()

        for copy in self.kept():
            copy.wait()


EXCHANGE_SEMS = [DMA((2,)), DMA((2, 32)), DMA((2, 32))]


def gather_kernel(
    slab,
    own,
    main,
    extra,
    full,
    items,
    mains,
    extras,
    relay,
    local,
    send,
    recv,
    near_send,
    near_recv,
    seq_local,
    seq_send,
    seq_recv,
    *exchange_sems,
):
    x, y, z, core = place()
    at = {"x": x, "y": y, "z": z}
    sibling = device(x, y, z, 1 - core)

    def moved(axis, by):
        return dict(at, **{axis: rem(at[axis] + by, 4)})

    def who(spot):
        return device(spot["x"], spot["y"], spot["z"], core)

    greet_peers([who(moved(axis, by)) for axis in "xyz" for by in (1, 3)] + [sibling])
    packets = Exchange((main, extra), (mains, extras), *exchange_sems)

    def block(spot, whole, first, width):
        every = slice(None)
        row = every if "y" in whole else spot["y"]
        depth = every if "z" in whole else spot["z"]
        near, far = every, every
        if "x" not in whole:
            near, far = rem(spot["x"], 2), div(spot["x"], 2)
        return full.at[row, near, depth, far, core, :, pl.ds(first, width)]

    near = []

    def share(ref):
        k = len(near)
        copy = remote(ref, ref, near_send.at[k], near_recv.at[k], sibling)
        copy.start()
        near.append(copy)

    own_place = full.at[y, rem(x, 2), z, div(x, 2), core]
    mine = pltpu.make_async_copy(slab, own_place, local)
    mine.start()
    sems = (seq_local, seq_send, seq_recv)
    state = seq_gather_start(own, items, relay, sems)
    packets.keep()
    mine.wait()
    share(own_place)
    sent = []
    for stage in range(3):
        steps = []
        for part in range(3):
            axis, whole = ORDERS[part][stage], ORDERS[part][:stage]
            first, width = PARTS[part]
            near_half = 768
            k = (part * 3 + stage) * 4
            right, left = who(moved(axis, 1)), who(moved(axis, 3))
            here = block(at, whole, first, width)
            there_left, there_right = moved(axis, 3), moved(axis, 1)
            part_left = block(there_left, whole, first, near_half)
            part_right = block(there_right, whole, first + near_half, width - near_half)
            copies = [
                remote(here, here, send.at[k], recv.at[k], right),
                remote(here, here, send.at[k + 1], recv.at[k + 1], left),
                remote(part_left, part_left, send.at[k + 2], recv.at[k + 2], right),
                remote(part_right, part_right, send.at[k + 3], recv.at[k + 3], left),
            ]
            copies[0].start()
            copies[1].start()
            opposite = moved(axis, 2)
            steps.append(
                (
                    copies,
                    [
                        block(there_left, whole, first, width),
                        block(there_right, whole, first, width),
                        block(opposite, whole, first, near_half),
                        block(opposite, whole, first + near_half, width - near_half),
                    ],
                )
            )
            sent.extend(copies)
        packets.start(*((1, 11), (11, 22), (22, 32))[stage])
        for copies, arrived in steps:
            for k in range(2):
                copies[k].wait_recv()
                copies[k + 2].start()
                share(arrived[k])
        for copies, arrived in steps:
            for k in range(2, 4):
                copies[k].wait_recv()
                share(arrived[k])
    seq_gather_finish(state, items, relay, sems)
    packets.finish()
    for copy in near:
        copy.wait_recv()
    for copy in sent + near:
        copy.wait_send()


def gather_all(slab, own, main, extra):
    return pl.pallas_call(
        gather_kernel,
        out_shape=(
            jax.ShapeDtypeStruct((4, 2, 4, 2, 2, 8, SLAB), BF16),
            jax.ShapeDtypeStruct((2, 4, 16, 8, D), BF16),
            jax.ShapeDtypeStruct((32, 2, 8, D), BF16),
            jax.ShapeDtypeStruct((32, 2, 8, 256), BF16),
        ),
        in_specs=[ANY] * 4,
        out_specs=(ANY,) * 4,
        scratch_shapes=[
            pltpu.VMEM((2, 16, 8, D), BF16),
            DMA(()),
            DMA((36,)),
            DMA((36,)),
            DMA((37,)),
            DMA((37,)),
            DMA(()),
            DMA((7,)),
            DMA((7,)),
            *EXCHANGE_SEMS,
        ],
        compiler_params=params(0, 32),
        cost_estimate=cost(90 << 20),
    )(slab, own, main, extra)


def items_kernel(own, full, relay, local, send, recv):
    x, y, z, core = place()
    greet(
        [
            device(rem(x + 1, 4), y, z, core),
            device(rem(x + 3, 4), y, z, core),
            device(x, y, z, 1 - core),
        ]
    )
    sems = (local, send, recv)
    state = seq_gather_start(own, full, relay, sems)
    seq_gather_finish(state, full, relay, sems)


def gather_items(own):
    return pl.pallas_call(
        items_kernel,
        out_shape=jax.ShapeDtypeStruct((2, 4, 16, 8, D), BF16),
        in_specs=[ANY],
        out_specs=ANY,
        scratch_shapes=[pltpu.VMEM((2, 16, 8, D), BF16), DMA(()), DMA((7,)), DMA((7,))],
        compiler_params=params(1, 32),
        cost_estimate=cost(20 << 20),
    )(own)


def grads_kernel(
    heads,
    rest,
    part,
    main,
    extra,
    mine,
    other,
    small,
    wide,
    mains,
    extras,
    own,
    got,
    relay,
    first_in,
    first_sum,
    second_in,
    total,
    own_local,
    near_send,
    near_recv,
    relay_send,
    relay_recv,
    first_local,
    first_send,
    first_recv,
    second_send,
    second_recv,
    last_local,
    last_send,
    last_recv,
    *exchange_sems,
):
    x, y, z, core = place()
    my_dp, my_seq = device(x, y, z, core)
    sibling = device(x, y, z, 1 - core)
    right, left = device(rem(x + 1, 4), y, z, core), device(rem(x + 3, 4), y, z, core)
    here = div(x, 2)
    away = 1 - here

    greet_peers([(my_dp, rem(my_seq + step, 4)) for step in range(1, 4)] + [right, left])

    shares = []
    for k, side in enumerate((away, here)):
        shares.append(
            (
                remote(
                    part.at[:, side * 2 + 1 - core],
                    got.at[k],
                    near_send.at[k],
                    near_recv.at[k],
                    sibling,
                ),
                pltpu.make_async_copy(part.at[:, side * 2 + core], own.at[k], own_local.at[k]),
            )
        )
        for copy in shares[k]:
            copy.start()

    near, every = rem(x, 2), slice(None)
    sizes = (4, 4, 2)
    low, high = pl.ds(0, THIRD), pl.ds(THIRD, THIRD)

    def piece(index, step):
        if index == 0:
            return heads.at[rem(y + step, 4), :, :, :, :, low]
        if index == 1:
            return heads.at[:, :, rem(z + step, 4), :, :, high]
        return rest.at[:, rem(near + step, 2)]

    def along(index, step):
        if index == 0:
            return device(x, rem(y + step, 4), z, core)
        if index == 1:
            return device(x, y, rem(z + step, 4), core)
        return device(here * 2 + rem(near + step, 2), y, z, core)

    firsts, keeps = [], []
    for index in range(3):
        for step in range(sizes[index]):
            k = index * 4 + step
            if step == 0:
                copy = pltpu.make_async_copy(
                    piece(index, 0), first_in[index].at[0], first_local.at[index]
                )
                keeps.append(copy)
            else:
                copy = remote(
                    piece(index, step),
                    first_in[index].at[step],
                    first_send.at[k],
                    first_recv.at[k],
                    along(index, step),
                )
                firsts.append((index, copy))
            copy.start()
    packets = Exchange((main, extra), (mains, extras), *exchange_sems)
    packets.start(1, 32)
    packets.keep()

    shares[0][1].wait()
    shares[0][0].wait_recv()
    hops = [
        remote(own.at[0, 0], relay.at[0], relay_send.at[0], relay_recv.at[0], right),
        remote(own.at[0, 1], relay.at[1], relay_send.at[1], relay_recv.at[1], left),
        remote(relay.at[0], other.at[0], relay_send.at[2], relay_recv.at[2], right),
        remote(relay.at[1], other.at[1], relay_send.at[3], relay_recv.at[3], left),
    ]
    for item in range(2):

        @pl.loop(0, 8)
        def _(row):
            rows = pl.ds(row * 2, 2)
            summed = own[0, item, rows].astype(F32) + got[0, item, rows].astype(F32)
            own[0, item, rows] = summed.astype(BF16)

        hops[item].start()
    shares[1][1].wait()
    shares[1][0].wait_recv()
    for item in range(2):

        @pl.loop(0, 8)
        def _(row):
            rows = pl.ds(row * 2, 2)
            mine[item, rows] = own[1, item, rows].astype(F32) + got[1, item, rows].astype(F32)

    for item in range(2):
        hops[item].wait_recv()
        hops[2 + item].start()

    def to_second(index, k):
        if index == 0:
            a, b = rem(near + div(k, 4), 2), rem(z + rem(k, 4), 4)
            return (a, b), device(here * 2 + a, y, b, core)
        if index == 1:
            a, b = rem(y + rem(k, 4), 4), rem(near + div(k, 4), 2)
            return (a, b), device(here * 2 + b, a, z, core)
        a, b = rem(y + div(k, 4), 4), rem(z + rem(k, 4), 4)
        return (a, b), device(x, a, b, core)

    def second(index, k):
        spot, to = to_second(index, k)
        slot = index * 8 + k
        return remote(
            first_sum[index].at[spot],
            second_in.at[slot],
            second_send.at[slot],
            second_recv.at[slot],
            to,
        )

    counts = (8, 8, 16)
    for index in range(3):
        keeps[index].wait()
        for which, copy in firsts:
            if which == index:
                copy.wait_recv()
        held, summed = first_in[index], first_sum[index]
        rows, columns = summed.shape[0], summed.shape[1]

        @pl.loop(0, rows)
        def _(a):
            for b in range(columns):
                value = held[0, a, b].astype(F32)
                for step in range(1, sizes[index]):
                    value = value + held[step, a, b].astype(F32)
                summed[a, b] = value.astype(BF16)

        @pl.loop(1, counts[index])
        def _(k):
            second(index, k).start()

    for index in range(3):
        columns = pl.ds(index * THIRD, THIRD)
        total[:, :, columns] = first_sum[index][to_second(index, jnp.int32(0))[0]].astype(F32)

        @pl.loop(1, counts[index])
        def _(k):
            second(index, k).wait_recv()
            total[:, :, columns] += second_in[index * 8 + k].astype(F32)

    columns = 3 * 256 + 128
    last = []
    for step in range(1, 4):
        seq = rem(my_seq + step, 4)
        copy = remote(
            total.at[seq, :, pl.ds(0, columns)],
            small.at[my_seq],
            last_send.at[step],
            last_recv.at[step],
            (my_dp, seq),
        )
        copy.start()
        last.append(copy)
    keep = pltpu.make_async_copy(
        total.at[my_seq, :, pl.ds(0, columns)],
        small.at[my_seq],
        last_local,
    )
    keep.start()
    wide[...] = total[:, :, columns:]
    keep.wait()
    for copy in last:
        copy.wait_recv()
    for item in range(2):
        hops[2 + item].wait_recv()
    packets.finish()
    for copy in last + hops + [share[0] for share in shares]:
        copy.wait_send()

    for _, copy in firsts:
        copy.wait_send()
    for index in range(3):

        @pl.loop(1, counts[index])
        def _(k):
            second(index, k).wait_send()


def reduce_grads(heads, rest, part, main, extra):
    columns = 3 * 256 + 128
    return pl.pallas_call(
        grads_kernel,
        out_shape=(
            jax.ShapeDtypeStruct((2, 16, 8, D), F32),
            jax.ShapeDtypeStruct((2, 16, 8, D), BF16),
            jax.ShapeDtypeStruct((4, 8, columns), F32),
            jax.ShapeDtypeStruct((4, 8, 256), F32),
            jax.ShapeDtypeStruct((32, 2, 8, D), BF16),
            jax.ShapeDtypeStruct((32, 2, 8, 256), BF16),
        ),
        in_specs=[ANY] * 5,
        out_specs=(VMEM, ANY, VMEM, VMEM, ANY, ANY),
        scratch_shapes=[
            pltpu.VMEM((2, 2, 16, 8, D), BF16),
            pltpu.VMEM((2, 2, 16, 8, D), BF16),
            pltpu.VMEM((2, 16, 8, D), BF16),
            [
                pltpu.VMEM((4, 2, 4, 4, 8, THIRD), BF16),
                pltpu.VMEM((4, 4, 2, 4, 8, THIRD), BF16),
                pltpu.VMEM((2, 4, 4, 4, 8, THIRD), BF16),
            ],
            [
                pltpu.VMEM((2, 4, 4, 8, THIRD), BF16),
                pltpu.VMEM((4, 2, 4, 8, THIRD), BF16),
                pltpu.VMEM((4, 4, 4, 8, THIRD), BF16),
            ],
            pltpu.VMEM((32, 4, 8, THIRD), BF16),
            pltpu.VMEM((4, 8, GRAD), F32),
            DMA((2,)),
            DMA((2,)),
            DMA((2,)),
            DMA((4,)),
            DMA((4,)),
            DMA((3,)),
            DMA((12,)),
            DMA((12,)),
            DMA((32,)),
            DMA((32,)),
            DMA(()),
            DMA((4,)),
            DMA((4,)),
            *EXCHANGE_SEMS,
        ],
        compiler_params=params(4, 48),
        cost_estimate=cost(60 << 20),
    )(heads, rest, part, main, extra)


NT = (((1,), (1,)), ((), ()))
TN = (((0,), (0,)), ((), ()))


def dot(a, b, dims=None):
    if dims is None:
        return jnp.dot(a, b, preferred_element_type=F32)
    return lax.dot_general(a, b, dims, preferred_element_type=F32)


def bias_rows(window):
    return pltpu.roll(
        jnp.broadcast_to(window, (ROWS, 640)), 640 - 127, 1, stride=1, stride_axis=0
    )[:, :LENGTH]


def flat(rows):
    return rows.astype(F32).reshape(rows.shape[0] * 8, 128).astype(BF16)


def tiled(rows):
    return rows.reshape(rows.shape[0] // 8, 8, 128).astype(BF16)


def softmax(scores):
    powers = jnp.exp(scores - jnp.max(scores, -1, keepdims=True))
    return powers * (1.0 / jnp.sum(powers, -1, keepdims=True))


def forward_kernel(window, query, key, value, mixed):
    low = lax.broadcasted_iota(jnp.int32, (ROWS, 128), 1) < SIZE
    biases = [bias_rows(window[0, head : head + 1]) for head in range(2)]
    for item in range(2):
        queries = query[item].astype(F32).reshape(ROWS, 128) * SIZE**-0.5
        keys, values = flat(key[item]), flat(value[item])
        results = []
        for head in range(2):
            own = low if head == 0 else ~low
            one = jnp.where(own, queries, 0.0).astype(BF16)
            scores = dot(one, keys, NT) + biases[head]
            results.append(dot(softmax(scores).astype(BF16), values))
        mixed[item] = tiled(jnp.where(low, results[0], results[1]))


def attend(windows, query, key_value):
    def block(rows, first=0):
        return pl.BlockSpec((2, rows // 8, 8, 128), lambda pair: (0, 0, 0, first + pair))

    return pl.pallas_call(
        forward_kernel,
        grid=(HEADS // 2,),
        out_shape=jax.ShapeDtypeStruct((2, ROWS // 8, 8, D), BF16),
        in_specs=[
            pl.BlockSpec((1, 2, 640), lambda pair: (pair, 0, 0)),
            block(ROWS),
            block(LENGTH),
            block(LENGTH, HEADS // 2),
        ],
        out_specs=block(ROWS),
        compiler_params=pltpu.CompilerParams(vmem_limit_bytes=32 << 20),
        cost_estimate=cost(12 << 20, 4 << 30),
    )(windows, query, key_value, key_value)


def backward_kernel(windows, query, key, value, grad, mixed, dquery, dkey, dvalue, dbias):
    low = lax.broadcasted_iota(jnp.int32, (LENGTH, 128), 1) < SIZE
    keys, values = flat(key[0]), flat(value[0])
    all_queries = query[0].astype(F32).reshape(LENGTH, 128) * SIZE**-0.5
    all_grads = grad[0].astype(F32).reshape(LENGTH, 128)
    blocks = LENGTH // ROWS
    results = []
    for head in range(2):
        own = low if head == 0 else ~low
        queries = jnp.where(own, all_queries, 0.0).astype(BF16)
        grads = jnp.where(own, all_grads, 0.0).astype(BF16)
        bias = jnp.concatenate(
            [bias_rows(windows[0, head, block : block + 1]) for block in range(blocks)], 0
        )
        probs = softmax(dot(queries, keys, NT) + bias)
        low_probs = probs.astype(BF16)
        dprobs = dot(grads, values, NT)
        dscores = probs * (dprobs - jnp.sum(probs * dprobs, -1, keepdims=True))
        low_scores = dscores.astype(BF16)
        results.append(
            (
                dot(low_probs, values),
                dot(low_scores, keys) * SIZE**-0.5,
                dot(low_scores, queries, TN),
                dot(low_probs, grads, TN),
            )
        )
        diagonal = jnp.zeros((1, 1024), F32)
        for block in range(blocks):
            sums = jnp.concatenate(
                [
                    low_scores[block * ROWS : block * ROWS + ROWS].astype(F32),
                    jnp.zeros((ROWS, 128), F32),
                ],
                axis=1,
            )
            count = ROWS
            while count > 1:
                count //= 2
                sums = pltpu.roll(sums[:count], count, 1) + sums[count:]
            first = LENGTH - ROWS - block * ROWS
            pieces = [sums]
            if first:
                pieces.insert(0, jnp.zeros((1, first), F32))
            if first + 640 < 1024:
                pieces.append(jnp.zeros((1, 1024 - 640 - first), F32))
            diagonal = diagonal + jnp.concatenate(pieces, axis=1)
        dbias[0, 0, head : head + 1] = diagonal
    for ref, one, two in zip((mixed, dquery, dkey, dvalue), *results):
        ref[0] = tiled(jnp.where(low, one, two))


def attend_back(windows, query, key, value, grad):
    block = pl.BlockSpec((1, LENGTH // 8, 8, 128), lambda pair, item: (item, 0, 0, pair))
    shape = jax.ShapeDtypeStruct((2, LENGTH // 8, 8, 256), BF16)
    return pl.pallas_call(
        backward_kernel,
        grid=(2, 2),
        out_shape=(shape,) * 4 + (jax.ShapeDtypeStruct((2, 2, 2, 1024), F32),),
        in_specs=[
            pl.BlockSpec((1, 2, 4, 640), lambda pair, item: (pair, 0, 0, 0)),
            block,
            block,
            block,
            block,
        ],
        out_specs=(block,) * 4
        + (pl.BlockSpec((1, 1, 2, 1024), lambda pair, item: (item, pair, 0, 0)),),
        compiler_params=pltpu.CompilerParams(vmem_limit_bytes=48 << 20),
        cost_estimate=cost(12 << 20, 8 << 30),
    )(windows, query, key, value, grad)


def rows_of(packets):
    count, width = packets.shape[0], packets.shape[-1]
    return packets.astype(F32).reshape(count * 16, width).astype(BF16)


def packets_of(rows):
    return rows.astype(F32).reshape(rows.shape[0] // 16, 2, 8, rows.shape[1]).astype(BF16)


def expert_rows(rows, grads, gates, gate_w, up_w, down_w, dgate, dup, ddown):
    gate_pre = dot(rows, gate_w[...], NT)
    up_pre = dot(rows, up_w[...], NT)
    square = gate_pre * gate_pre
    root = math.sqrt(2 / math.pi)
    tanh = jnp.tanh(root * gate_pre * (1.0 + 0.044715 * square))
    half = 0.5 * (1.0 + tanh)
    value = gate_pre * half
    slope = half + (0.5 * root) * gate_pre * (1.0 - tanh * tanh) * (1.0 + 3 * 0.044715 * square)
    active = (value * up_pre).astype(BF16)
    out = dot(active, down_w[...])
    grads = grads.astype(F32)
    grad_gates = jnp.sum(out * grads, -1, keepdims=True)
    grad_out = (gates * grads).astype(BF16)
    grad_active = dot(grad_out, down_w[...], NT)
    grad_gate = (grad_active * up_pre * slope).astype(BF16)
    grad_up = (grad_active * value).astype(BF16)
    grad_rows = dot(grad_gate, gate_w[...]) + dot(grad_up, up_w[...])
    dgate[...] += dot(grad_gate, rows, TN)
    dup[...] += dot(grad_up, rows, TN)
    ddown[...] += dot(active, grad_out, TN)
    return out.astype(BF16), grad_rows.astype(BF16), grad_gates


def moe_kernel(
    main,
    tail,
    grads_main,
    grads_extra,
    gate_w,
    up_w,
    down_w,
    back_main,
    back_tail,
    out_main,
    out_extra,
    dgate,
    dup,
    ddown,
    own_main,
    own_tail,
    sib_main,
    sib_tail,
    grad_main,
    grad_extra,
    res_main,
    res_extra,
    part_main,
    part_tail,
    give_main,
    give_tail,
    got_main,
    got_tail,
    keep_sem,
    send,
    recv,
    near_send,
    near_recv,
    grad_sem,
    res_sem,
    give_send,
    give_recv,
    back_keep,
    back_send,
    back_recv,
):
    x, y, z, core = place()
    my_dp = device(x, y, z, core)[0]
    sibling = device(x, y, z, 1 - core)
    greet_chips()
    slabs, own, sib = (main, tail), (own_main, own_tail), (sib_main, sib_tail)
    part, give, got = (part_main, part_tail), (give_main, give_tail), (got_main, got_tail)
    back = (back_main, back_tail)
    per = 8

    def packet(k):
        to = device(*chips(k)[0], core)
        return [
            remote(slabs[i].at[to[0]], own[i].at[k], send.at[i, k], recv.at[i, k], to)
            for i in range(2)
        ]

    def keep():
        return [
            pltpu.make_async_copy(slabs[i].at[my_dp], own[i].at[0], keep_sem.at[i])
            for i in range(2)
        ]

    def share(k):
        return [
            remote(own[i].at[k], sib[i].at[k], near_send.at[i, k], near_recv.at[i, k], sibling)
            for i in range(2)
        ]

    def arrive(block):
        @pl.loop(0, per)
        def _(j):
            k = block * per + j

            @pl.when(k > 0)
            def _():
                for copy in packet(k):
                    copy.wait_recv()

            for copy in share(k):
                copy.start()

    def fetches(block, j):
        slot = rem(block, 2)
        copies = []
        for side in range(2):
            dp, seq = device(*chips(block * per + j)[1], core if side == 0 else 1 - core)
            for i, (source, held) in enumerate(((grads_main, grad_main), (grads_extra, grad_extra))):
                place_at = side * per + j
                copies.append(
                    pltpu.make_async_copy(
                        source.at[seq, dp], held.at[slot, place_at], grad_sem.at[i, slot, place_at]
                    )
                )
        return copies

    def results(block, j):
        slot = rem(block, 2)
        copies = []
        for side in range(2):
            dp, seq = device(*chips(block * per + j)[1], core if side == 0 else 1 - core)
            for i, (held, target) in enumerate(((res_main, out_main), (res_extra, out_extra))):
                place_at = side * per + j
                copies.append(
                    pltpu.make_async_copy(
                        held.at[slot, place_at], target.at[seq, dp], res_sem.at[i, slot, place_at]
                    )
                )
        return copies

    def each(copies, block, act):
        @pl.loop(0, per)
        def _(j):
            for copy in copies(block, j):
                act(copy)

    def hand(block):
        some = pl.ds(block * per, per)
        return [
            remote(
                give[i].at[some],
                got[i].at[some],
                give_send.at[i, block],
                give_recv.at[i, block],
                sibling,
            )
            for i in range(2)
        ]

    def reply(k):
        to = device(*chips(k)[1], core)
        return [
            remote(
                part[i].at[k], back[i].at[div(x, 2), my_dp], back_send.at[i, k], back_recv.at[i, k], to
            )
            for i in range(2)
        ]

    def keep_back():
        return [
            pltpu.make_async_copy(
                part[i].at[0], back[i].at[div(x, 2), my_dp], back_keep.at[i]
            )
            for i in range(2)
        ]

    def finish(block):
        for copy in hand(block):
            copy.wait_recv()

        @pl.loop(0, per)
        def _(j):
            k = block * per + j
            for i in range(2):
                part[i][k] = (part[i][k].astype(F32) + got[i][k].astype(F32)).astype(BF16)

            @pl.when(k > 0)
            def _():
                for copy in reply(k):
                    copy.start()

            @pl.when(k == 0)
            def _():
                for copy in keep_back():
                    copy.start()

    def work(block):
        slot = rem(block, 2)
        some = pl.ds(block * per, per)
        target = lax.broadcasted_iota(jnp.int32, (64, 256), 0)
        source = lax.broadcasted_iota(jnp.int32, (64, 256), 1)
        picks = [(source == 4 * target + m).astype(F32).astype(BF16) for m in range(4)]

        def whole(extra):
            return jnp.concatenate([dot(pick, extra).astype(BF16) for pick in picks], 1)

        def quarters(rows):
            pieces = [
                dot(picks[m], rows[:, 256 * m : 256 * m + 256], TN) for m in range(4)
            ]
            return pieces[0] + pieces[1] + pieces[2] + pieces[3]

        tails = jnp.concatenate([rows_of(own_tail[some]), rows_of(sib_tail[some])], 0)
        rows = jnp.concatenate(
            [rows_of(own_main[some]), rows_of(sib_main[some]), whole(tails[:, :256])], 0
        )
        grads = jnp.concatenate(
            [rows_of(grad_main[slot]), whole(rows_of(grad_extra[slot]))], 0
        )
        scalars = jnp.concatenate([tails[:, 256:].astype(F32), dot(picks[0], tails[:, 256:])], 0)
        first = lax.broadcasted_iota(jnp.int32, (320, 1), 0) < 256
        gates = jnp.where(
            first,
            scalars[:, 0:1] + scalars[:, 1:2],
            scalars[:, 2:3] + scalars[:, 3:4],
        )
        out, grad_rows, grad_gates = expert_rows(
            rows, grads, gates, gate_w, up_w, down_w, dgate, dup, ddown
        )
        res_main[slot] = packets_of(out[:256])
        res_extra[slot] = packets_of(quarters(out[256:]))
        lane = lax.broadcasted_iota(jnp.int32, (320, 128), 1)
        lanes = jnp.where(lane == jnp.where(first, 0, 1), grad_gates, 0.0)
        extra_lanes = lanes[256:].astype(BF16)
        aux = lanes[:256] + (
            dot(picks[0], extra_lanes, TN)
            + dot(picks[1], extra_lanes, TN)
            + dot(picks[2], extra_lanes, TN)
            + dot(picks[3], extra_lanes, TN)
        )
        ends = jnp.concatenate([quarters(grad_rows[256:]), aux], 1)
        part_main[some] = packets_of(grad_rows[:128])
        give_main[some] = packets_of(grad_rows[128:256])
        part_tail[some] = packets_of(ends[:128])
        give_tail[some] = packets_of(ends[128:])

    for copy in keep():
        copy.start()

    @pl.loop(1, 64)
    def _(k):
        for copy in packet(k):
            copy.start()

    each(fetches, 0, lambda copy: copy.start())
    dgate[...] = jnp.zeros_like(dgate)
    dup[...] = jnp.zeros_like(dup)
    ddown[...] = jnp.zeros_like(ddown)
    for copy in keep():
        copy.wait()
    arrive(0)
    blocks = 64 // per

    @pl.loop(0, blocks)
    def _(block):
        @pl.when(block < blocks - 1)
        def _():
            each(fetches, block + 1, lambda copy: copy.start())
            arrive(block + 1)

        @pl.loop(0, per)
        def _(j):
            for copy in share(block * per + j):
                copy.wait_recv()

        each(fetches, block, lambda copy: copy.wait())

        @pl.when(block >= 2)
        def _():
            each(results, block - 2, lambda copy: copy.wait())

        work(block)
        each(results, block, lambda copy: copy.start())
        for copy in hand(block):
            copy.start()

        @pl.when(block >= 1)
        def _():
            finish(block - 1)

    finish(blocks - 1)
    for block in (blocks - 2, blocks - 1):
        each(results, block, lambda copy: copy.wait())

    @pl.loop(0, blocks)
    def _(block):
        for copy in hand(block):
            copy.wait_send()

    @pl.loop(0, 64)
    def _(k):
        for copy in share(k):
            copy.wait_send()

        @pl.when(k > 0)
        def _():
            for copy in packet(k):
                copy.wait_send()
            for copy in reply(k):
                copy.wait_recv()
                copy.wait_send()

    for copy in keep_back():
        copy.wait()


def run_experts(main, tail, grads_main, grads_extra, gate_w, up_w, down_w):
    wide = gate_w.shape[0]
    grad = jax.ShapeDtypeStruct((wide, D), F32)

    def pair(count):
        return [pltpu.VMEM((count, 2, 8, D), BF16), pltpu.VMEM((count, 2, 8, TAIL), BF16)]

    staged = [pltpu.VMEM((2, 16, 2, 8, D), BF16), pltpu.VMEM((2, 16, 2, 8, 256), BF16)]
    return pl.pallas_call(
        moe_kernel,
        out_shape=(
            jax.ShapeDtypeStruct((2, 32, 2, 8, D), BF16),
            jax.ShapeDtypeStruct((2, 32, 2, 8, TAIL), BF16),
            jax.ShapeDtypeStruct((4, 32, 2, 8, D), BF16),
            jax.ShapeDtypeStruct((4, 32, 2, 8, 256), BF16),
            grad,
            grad,
            grad,
        ),
        in_specs=[ANY] * 4 + [VMEM] * 3,
        out_specs=(ANY,) * 4 + (VMEM,) * 3,
        scratch_shapes=pair(64)
        + pair(64)
        + staged
        + staged
        + pair(64)
        + pair(64)
        + pair(64)
        + [DMA((2,))]
        + [DMA((2, 64))] * 4
        + [DMA((2, 2, 16))] * 2
        + [DMA((2, 8))] * 2
        + [DMA((2,))]
        + [DMA((2, 64))] * 2,
        compiler_params=params(2, 60),
        cost_estimate=cost(90 << 20, 33 << 30),
    )(main, tail, grads_main, grads_extra, gate_w, up_w, down_w)


def rms_forward(values, gain):
    factor = lax.rsqrt(jnp.mean(values * values, -1, keepdims=True) + EPSILON)
    normed = values * factor
    return (normed, factor, normed * gain)


def rms_values(grad_output, normed, factor, gain):
    grad_normed = grad_output * gain
    return factor * (grad_normed - normed * jnp.mean(grad_normed * normed, -1, keepdims=True))


def split(values):
    high = values.astype(BF16)
    return high, (values - high.astype(F32)).astype(BF16)


def body(
    layer_in,
    w_query,
    w_key,
    w_value,
    w_out,
    norm_attn,
    norm_moe,
    rel_table,
    w_router,
    expert_gate,
    expert_up,
    expert_down,
    routes,
    rel_bucket,
    cotangent,
):
    tokens = 2 * ROWS
    seq = lax.axis_index("seq")

    route_flat = routes.reshape(tokens, 2)
    expert_ids = jnp.arange(EXPERTS, dtype=jnp.int32)
    choose_hot = route_flat[:, :, None] == expert_ids[None, None, :]
    order_hot = choose_hot.transpose(1, 0, 2).reshape(2 * tokens, EXPERTS).astype(jnp.int32)
    earlier = jnp.cumsum(order_hot, 0) - order_hot
    slot_order = jnp.sum(earlier * order_hot, -1)
    dropped = jnp.sum(order_hot * (slot_order >= CAP)[:, None].astype(jnp.int32), 0)
    tallies = jnp.stack([jnp.sum(order_hot, 0), dropped])
    slots = slot_order.reshape(2, tokens).transpose(1, 0)
    columns = jnp.arange(EXPERTS * MAIN, dtype=jnp.int32)
    main_place = jnp.where(slots < MAIN, route_flat * MAIN + slots, -1)
    hot_main = main_place[:, :, None] == columns[None, None, :]
    extra_place = jnp.where(
        (slots >= MAIN) & (slots < CAP), route_flat * 4 + slots - MAIN, -1
    )
    hot_extra = extra_place[:, :, None] == (columns // 4)[None, None, :]
    quarter = jnp.arange(4, dtype=jnp.int32)
    quarter_hot = quarter[:, None] == (columns % 4)[None, :]

    def spread(values_k):
        hot_m = hot_main.astype(BF16)
        hot_x = (hot_extra[None] & quarter_hot[:, None, None, :]).astype(BF16)
        main = jnp.einsum("tkc,td->cd", hot_m, values_k, preferred_element_type=F32)
        extra = jnp.einsum(
            "mtkc,tmd->cd", hot_x, values_k.reshape(tokens, 4, 256), preferred_element_type=F32
        )
        return main.astype(BF16), extra.astype(BF16)

    slab = jnp.concatenate(
        [
            w_query,
            w_key,
            w_value,
            w_out,
            w_router,
            norm_attn[:, None],
            norm_moe[:, None],
            jnp.pad(rel_table[None], ((0, 7), (0, 0))),
            jnp.pad(tallies.astype(BF16), ((0, 6), (0, 0))),
            jnp.zeros((8, 186), BF16),
        ],
        1,
    )
    grad_main, grad_extra = spread(cotangent.reshape(tokens, D))
    full, items, grads_main, grads_extra = gather_all(
        slab,
        layer_in.reshape(2, 16, 8, D),
        grad_main.reshape(EXPERTS, 2, 8, D),
        grad_extra.reshape(EXPERTS, 2, 8, 256),
    )

    full = full.reshape(D, SLAB)
    full_query, full_kv, full_out = full[:, :D], full[:, D : 3 * D], full[:, 3 * D : 4 * D]
    smalls = full[:, 4 * D :]
    full_router = smalls[:, 0:32]
    gain_attn = smalls[:, 32].astype(F32)
    gain_moe = smalls[:, 33].astype(F32)
    smalls = smalls.reshape(128, 8, 256)
    table = smalls[:, 0, 34:38].reshape(BUCKETS, HEADS)
    totals = jnp.sum(smalls[:, 0:2, 38:70].astype(F32), 0).astype(jnp.int32)

    inputs = layer_in.astype(F32).reshape(tokens, D)
    own_hidden = rms_forward(inputs, gain_attn)[2].astype(BF16)
    all_inputs = items.astype(F32).reshape(4 * tokens, D)
    normed_one, factor_one, hidden_one = rms_forward(all_inputs, gain_attn)
    hidden_one = hidden_one.astype(BF16)
    query = dot(own_hidden, full_query).astype(BF16)
    kv_all = dot(hidden_one, full_kv).astype(BF16)
    bucket_hot = (rel_bucket[:, None] == jnp.arange(BUCKETS, dtype=jnp.int32)[None, :]).astype(BF16)
    offsets = jnp.einsum("ob,bh->ho", bucket_hot, table, preferred_element_type=F32)
    offsets = jnp.pad(offsets, ((0, 0), (0, 1)))
    windows = lax.dynamic_slice(offsets, (0, LENGTH - ROWS - seq * ROWS), (HEADS, 640))
    mixed = attend(
        windows.reshape(HEADS // 2, 2, 640),
        query.reshape(2, ROWS // 8, 8, D),
        kv_all.reshape(2, LENGTH // 8, 8, 2 * D),
    ).reshape(tokens, D)
    resid = inputs + dot(mixed, full_out)
    normed_two, factor_two, hidden_two = rms_forward(resid, gain_moe)
    hidden_two = hidden_two.astype(BF16)
    logits = dot(hidden_two, full_router)
    chosen = jnp.sum(jnp.where(choose_hot, logits[:, None, :], 0.0), -1)
    gates = jax.nn.softmax(chosen, -1)

    rows_main, rows_extra = spread(hidden_two)
    gate_main = jnp.sum(jnp.where(hot_main, gates[:, :, None], 0.0), (0, 1))
    gate_extra = jnp.sum(jnp.where(hot_extra, gates[:, :, None], 0.0), (0, 1))
    lanes = jnp.stack(split(gate_main) + split(gate_extra), -1)
    rows_tail = jnp.concatenate([rows_extra, jnp.pad(lanes, ((0, 0), (0, 124)))], -1)
    grads_main = lax.all_gather(grads_main, "seq", axis=0, tiled=False)
    grads_extra = lax.all_gather(grads_extra, "seq", axis=0, tiled=False)
    returned, returned_tail, out_main, out_extra, *expert_grads = run_experts(
        rows_main.reshape(EXPERTS, 2, 8, D),
        rows_tail.reshape(EXPERTS, 2, 8, TAIL),
        grads_main,
        grads_extra,
        expert_gate[0].T,
        expert_up[0].T,
        expert_down[0],
    )
    grad_gate, grad_up, grad_down = expert_grads[0].T, expert_grads[1].T, expert_grads[2]

    hot_both = jnp.sum(hot_main.astype(BF16), 1)
    hot_extra_both = jnp.sum(hot_extra.astype(BF16), 1)
    quarters = [hot_extra_both * quarter_hot[m][None, :].astype(BF16) for m in range(4)]
    back = returned.reshape(2 * EXPERTS * MAIN, D)
    back_tail = returned_tail.reshape(2 * EXPERTS * MAIN, TAIL)
    from_main = dot(jnp.concatenate([hot_both, hot_both], 1), back)
    from_extra = jnp.concatenate(
        [dot(jnp.concatenate([hot, hot], 1), back_tail[:, :256]) for hot in quarters], 1
    )
    grad_from_experts = from_main + from_extra
    returned_gates = back_tail[:, 256:258].astype(F32).reshape(2, EXPERTS * MAIN, 2)
    returned_gates = returned_gates[0] + returned_gates[1]
    grad_gates = jnp.sum(jnp.where(hot_main, returned_gates[:, 0], 0.0), -1) + 0.25 * jnp.sum(
        jnp.where(hot_extra, returned_gates[:, 1], 0.0), -1
    )

    grad_final = cotangent.astype(F32).reshape(tokens, D)
    grad_chosen = gates * (grad_gates - jnp.sum(gates * grad_gates, -1, keepdims=True))
    grad_logits = jnp.sum(jnp.where(choose_hot, grad_chosen[:, :, None], 0.0), 1).astype(BF16)
    grad_router_part = dot(hidden_two, grad_logits, TN)
    grad_hidden_two = grad_from_experts + dot(grad_logits, full_router, NT)
    grad_gain_moe = jnp.sum(grad_hidden_two * normed_two, 0)
    grad_resid = grad_final + rms_values(grad_hidden_two, normed_two, factor_two, gain_moe)
    grad_attended = gather_items(grad_resid.astype(BF16).reshape(2, 16, 8, D))
    grad_attended, out_main, out_extra = lax.optimization_barrier(
        (grad_attended, out_main, out_extra)
    )
    out_main = lax.psum_scatter(out_main, "seq", scatter_dimension=0, tiled=False)
    out_extra = lax.psum_scatter(out_extra, "seq", scatter_dimension=0, tiled=False)
    grad_attended = grad_attended.reshape(4 * tokens, D)

    first = seq * 256
    own_query, own_key, own_value = [
        lax.dynamic_slice(full, (0, index * D + first), (D, 256)) for index in range(3)
    ]
    own_out = lax.dynamic_slice(full, (first, 3 * D), (256, D))
    head_query = dot(hidden_one, own_query).astype(BF16)
    head_key = lax.dynamic_slice(kv_all, (0, first), (4 * tokens, 256))
    head_value = lax.dynamic_slice(kv_all, (0, D + first), (4 * tokens, 256))
    grad_mixed = dot(grad_attended, own_out, NT).astype(BF16)
    head_offsets = lax.dynamic_slice(offsets, (seq * 4, 0), (4, 1024))
    head_windows = jnp.stack(
        [
            head_offsets[:, LENGTH - ROWS - block * ROWS : LENGTH - ROWS - block * ROWS + 640]
            for block in range(4)
        ],
        1,
    ).reshape(2, 2, 4, 640)
    shape = (2, LENGTH // 8, 8, 256)
    head_mixed, dquery, dkey, dvalue, dbias = attend_back(
        head_windows,
        head_query.reshape(shape),
        head_key.reshape(shape),
        head_value.reshape(shape),
        grad_mixed.reshape(shape),
    )
    grad_offsets = jnp.sum(dbias, 0).reshape(4, 1024)[:, :1023]
    grad_table = jnp.einsum(
        "ob,ho->bh", bucket_hot.astype(F32), grad_offsets, precision=lax.Precision.HIGHEST
    )
    heads_grad = jnp.concatenate([dquery, dkey, dvalue], -1).reshape(4 * tokens, 768)
    own_weights = jnp.concatenate([own_query, own_key, own_value], 1)
    grad_qkv = dot(hidden_one, heads_grad, TN).astype(BF16).reshape(32, 32, 768)
    grad_out = dot(head_mixed.reshape(4 * tokens, 256), grad_attended, TN).astype(BF16)
    grad_out = grad_out.reshape(32, 8, 4, 256).transpose(0, 2, 1, 3).reshape(32, 32, 256)
    part_hidden = dot(heads_grad, own_weights, NT)
    grad_gain_attn = jnp.sum(part_hidden * normed_one, 0)
    table_lanes = (
        (jnp.arange(32, dtype=jnp.int32) == seq * 8)[None, :, None] * grad_table[:, None, :]
    )
    smalls_grad = jnp.concatenate(
        [
            grad_router_part.reshape(32, 32, 32),
            grad_gain_attn.reshape(32, 32, 1),
            grad_gain_moe.reshape(32, 32, 1),
            table_lanes,
            jnp.zeros((32, 32, 90), F32),
        ],
        -1,
    ).astype(BF16)
    rest = jnp.concatenate([smalls_grad, grad_out], -1)
    mine, other, small_sums, wide_sums, out_main, out_extra = reduce_grads(
        grad_qkv.reshape(4, 2, 4, 4, 8, 768),
        rest.reshape(4, 2, 4, 4, 8, 384),
        part_hidden.astype(BF16).reshape(2, 4, 16, 8, D),
        out_main,
        out_extra,
    )

    gated_main = split(jnp.sum(jnp.where(hot_main, gates[:, :, None], 0.0), 1))
    gated_extra = split(jnp.sum(jnp.where(hot_extra, gates[:, :, None], 0.0), 1))
    out_main = out_main.reshape(EXPERTS * MAIN, D)
    out_extra = out_extra.reshape(EXPERTS * MAIN, 256)
    moe_out = dot(
        jnp.concatenate(gated_main, 1), jnp.concatenate([out_main, out_main], 0)
    ) + jnp.concatenate(
        [
            dot(
                jnp.concatenate([part * quarter_hot[m][None, :].astype(BF16) for part in gated_extra], 1),
                jnp.concatenate([out_extra, out_extra], 0),
            )
            for m in range(4)
        ],
        1,
    )
    layer_out = (resid + moe_out).astype(BF16).reshape(2, ROWS, D)


    wide_sums = wide_sums.transpose(1, 0, 2).reshape(8, D)
    moves = [
        (dp * 4 + own, (8 * own + dp // 4) * 4 + dp % 4) for dp in range(32) for own in range(4)
    ]
    grad_out_own = lax.ppermute(wide_sums, ("dp", "seq"), moves)
    grad_weights = [
        small_sums[:, :, index * 256 : index * 256 + 256].transpose(1, 0, 2).reshape(8, D)
        for index in range(3)
    ]
    small_own = jnp.sum(small_sums[:, :, 768:], 0)
    grad_hidden_one = (mine + other.astype(F32)).reshape(tokens, D)
    own_normed, own_factor, _ = rms_forward(inputs, gain_attn)
    grad_in = grad_resid + rms_values(grad_hidden_one, own_normed, own_factor, gain_attn)
    return (
        layer_out,
        grad_in.reshape(2, ROWS, D),
        grad_weights[0],
        grad_weights[1],
        grad_weights[2],
        grad_out_own,
        small_own[:, 32],
        small_own[:, 33],
        small_own[0, 34:38],
        small_own[:, 0:32],
        grad_gate[None],
        grad_up[None],
        grad_down[None],
        totals,
    )


def solution(mesh):
    rows = P(("dp", "seq"), None)
    vector = P(("dp", "seq"))
    block = P("dp", "seq", None)
    wide = P("dp", None, "seq")
    return jax.shard_map(
        body,
        mesh=mesh,
        in_specs=(
            block,
            rows,
            rows,
            rows,
            rows,
            vector,
            vector,
            vector,
            rows,
            wide,
            wide,
            block,
            block,
            P(),
            block,
        ),
        out_specs=(
            block,
            block,
            rows,
            rows,
            rows,
            rows,
            vector,
            vector,
            vector,
            rows,
            wide,
            wide,
            block,
            P(),
        ),
        check_vma=False,
    )
```

time: 4170 us -> 491 us (0.12)
  waiting for transfers between devices: 3050 us -> 34.3 us
  local copies, waits for them, and re-layouts: 466 us -> 48.5 us
  blocking collectives: 398 us -> 0 us
  Pallas kernels: 0 us -> 311 us
  matrix products: 162 us -> 46.4 us
    reduce_scatter x7 -> x2, waiting for transfers between devices: 2600 us -> 21 us  [the longest x1 21 us: body(): lax.psum_scatter(out_main, 'seq', scatter_dimension=0, tiled=False)]
    pallas_call x0 -> x6, Pallas kernels: none -> 311 us  [the longest x1 132 us: run_experts(): pl.pallas_call(moe_kernel, out_shape=(jax.ShapeDtypeStruct((2, 32, 2, 8,...]
    all_gather x9 -> x2, waiting for transfers between devices: 314 us -> 12 us  [the longest x1 12 us: body(): grads_main = lax.all_gather(grads_main, 'seq', axis=0, tiled=False)]
    gather x2 -> x0, local copies, waits for them, and re-layouts: 261 us -> none  [body(): buckets = jnp.take(rel_bucket, offsets)]
    all_gather x1 -> x0, blocking collectives: 190 us -> none  [body(): lax.all_gather(w_router, ('dp', 'seq'), axis=0, tiled=True)]
    unnamed x2 -> x0, blocking collectives: 138 us -> none
    dot_general x36 -> x26, matrix products: 162 us -> 45.6 us  [the longest x15 23.2 us: dot(): return jnp.dot(a, b, preferred_element_type=F32)]
    unnamed x106 -> x156, local copies, waits for them, and re-layouts: 113 us -> 25.1 us
  transfers between devices with their start and end apart: 23 -> 5, of which waited for: 13 -> 2; matrix products, arithmetic and copies ran while one was open for 14% -> 14% of each run, Pallas kernels for 0% -> 7%
where the time goes in v1:
time: 491 us; the launch traced here: 486 us
  Pallas kernels  311 us (63%)
  local copies, waits for them, and re-layouts  48.5 us (10%)
  matrix products  46.4 us (9%)
  waiting for transfers between devices  34.3 us (7%)
  other arithmetic  25 us (5%)
  between operations  15 us (3%)
  starting transfers between devices  6.58 us (1%)
    pallas_call x1, Pallas kernels, run_experts(): pl.pallas_call(moe_kernel, out_shape=(jax.ShapeDtypeStruct((2, 32, 2, 8,...  132 us
    pallas_call x1, Pallas kernels, gather_all(): pl.pallas_call(gather_kernel, out_shape=(jax.ShapeDtypeStruct((4, 2, 4, 2...  61.1 us
    pallas_call x1, Pallas kernels, reduce_grads(): pl.pallas_call(grads_kernel, out_shape=(jax.ShapeDtypeStruct((2, 16, 8, D...  55.6 us
    pallas_call x1, Pallas kernels, gather_items(): pl.pallas_call(items_kernel, out_shape=jax.ShapeDtypeStruct((2, 4, 16, 8,...  27 us
    unnamed x156, local copies, waits for them, and re-layouts  25.1 us
    dot_general x15, matrix products, dot(): return jnp.dot(a, b, preferred_element_type=F32)  23.2 us
    pallas_call x1, Pallas kernels, attend_back(): pl.pallas_call(backward_kernel, grid=(2, 2), out_shape=(shape,) * 4 + (ja...  21.5 us
    reduce_scatter x1, waiting for transfers between devices, body(): lax.psum_scatter(out_main, 'seq', scatter_dimension=0, tiled=False)  21 us
  transfers between devices with their start and end apart: 5, of which 2 were waited for; matrix products, arithmetic and copies ran while one was open for 14% of the time, Pallas kernels for 7%

profile of v1, /device:TPU:5, one launch (start us, length us, event | category | flops | bytes accessed | tf_op | source)
XLA Modules:
  0.0 486.5 jit_solution(15254273863625061568)
XLA Ops:
  14.9 2.5 fusion.144
  20.5 61.1 %shard_map.254 = (bf16[4,2,4,2,2,8,4352]{6,5,4,3,2,1,0:T(8,128)(2,1)S(1)}, bf16[2,4,16,8,1024]{4,3,2,1,0:T(8,128)(2,1)S(1)}, bf16[32,2,8,1024]{3,2,1,0:T(8,128)(2,1)S(1)}, bf16[32,2,8,256]{3,2,1,0:T(8,128)(2,1)}) custom-call(bf16[8,4352]{1,0:T(8,128)(2,1)S(1)} %concatenate.74.slab, bf16[2,16,8,1024]{3,2,1,0:T(8,128)(2,1)S(1)} %bitcast.178, ...), custom_call_target="tpu_custom_call" | custom-call | bytes 94371840 | tf_op jit(solution)/shard_map/pallas_call | solution.py:319
  81.6 3.4 copy-done.3
  88.4 2.7 constant_dynamic-slice_fusion.1
  94.1 2.5 fusion.31
  98.4 4.7 fusion.2
  103.1 13.7 %shard_map.255 = bf16[2,16,8,1024]{3,2,1,0:T(8,128)(2,1)S(1)} custom-call(f32[8,2,640]{2,1,0:T(2,128)S(1)} %reshape.491.window, bf16[2,16,8,1024]{3,2,1,0:T(8,128)(2,1)S(1)} %bitcast.208, bf16[2,64,8,2048]{3,2,1,0:T(8,128)(2,1)S(1)} %bitcast.197, bf16[2,64,8,2048]{3,2,1,0:T(8,128)(2,1)S(1)} %bitcast.198), custom_call_target="tpu_custom_call" | custom-call | flops 4294967296 | bytes 12582912 | tf_op jit(solution)/shard_map/pallas_call | solution.py:690
  122.6 1.8 fusion.35
  125.2 1.9 copy.129
  127.4 1.8 broadcast_multiply_fusion.10
  132.0 12.0 %all-gather.5.cloned.1.call-done = bf16[128,2,8,1024]{3,2,1,0:T(8,128)(2,1)} async-done(((bf16[32,2,8,1024]{3,2,1,0:T(8,128)(2,1)}), bf16[128,2,8,1024]{3,2,1,0:T(8,128)(2,1)}) %all-gather.5.cloned.1.call-update) | async-done | bytes 4194320 | tf_op jit(solution)/shard_map/all_gather | solution.py:1263
  144.0 131.8 %shard_map.256 = (bf16[2,32,2,8,1024]{4,3,2,1,0:T(8,128)(2,1)}, bf16[2,32,2,8,384]{4,3,2,1,0:T(8,128)(2,1)}, bf16[4,32,2,8,1024]{4,3,2,1,0:T(8,128)(2,1)}, bf16[...) custom-call(bf16[32,2,8,1024]{3,2,1,0:T(8,128)(2,1)} %bitcast.221, ...), custom_call_target="tpu_custom_call" | custom-call | flops 35433480192 | bytes 94371840 | tf_op jit(solution)/shard_map/pallas_call | solution.py:1107
  276.8 2.0 fusion.62
  278.9 2.0 fusion.58
  283.7 2.5 convolution_add_fusion.1
  286.3 2.1 multiply_reduce_fusion.2
  289.4 27.0 %shard_map.257 = bf16[2,4,16,8,1024]{4,3,2,1,0:T(8,128)(2,1)S(1)} custom-call(bf16[2,16,8,1024]{3,2,1,0:T(8,128)(2,1)S(1)} %bitcast.183), custom_call_target="tpu_custom_call" | custom-call | bytes 20971520 | tf_op jit(solution)/shard_map/pallas_call | solution.py:361
  321.4 2.1 constant_dynamic-slice_fusion.2
  323.5 2.1 subtract_convert_fusion.1
  325.6 1.6 broadcast_multiply_fusion.6
  327.2 2.6 convolution_convert_fusion.5
  329.8 1.9 multiply_convert_fusion
  332.7 2.5 convolution_convert_fusion.4
  335.2 21.5 %shard_map.258 = (bf16[2,64,8,256]{3,2,1,0:T(8,128)(2,1)S(1)}, bf16[2,64,8,256]{3,2,1,0:T(8,128)(2,1)S(1)}, bf16[2,64,8,256]{3,2,1,0:T(8,128)(2,1)S(1)}, bf16[2,...) custom-call(f32[2,2,4,640]{3,2,1,0:T(4,128)S(1)} %pad_maximum_fusion.7.windows, bf16[2,64,8,256]{3,2,1,0:T(8,128)(2,1)S(1)} %bitcast.206, ...), custom_call_target="tpu_custom_call" | custom-call | flops 8589934592 | bytes 12582912 | tf_op jit(solution)/shard_map/pallas_call | solution.py:761
  359.0 3.2 fusion.140
  366.1 3.4 convolution_convert_fusion.3
  370.3 3.2 concatenate.89.rest
  373.5 4.4 convolution_convert_fusion
  377.9 21.0 %reduce-scatter.3.cloned.1.call-done = bf16[1,32,2,8,1024]{4,3,2,1,0:T(8,128)(2,1)} async-done(((bf16[4,32,2,8,1024]{4,3,2,1,0:T(8,128)(2,1)}), bf16[1,32,2,8,1024]{4,3,2,1,0:T(8,128)(2,1)}) %reduce-scatter.3.cloned.1.call-update) | async-done | bytes 1048592 | tf_op jit(solution)/shard_map/reduce_scatter | solution.py:1303
  401.1 55.6 %shard_map.259 = (f32[2,16,8,1024]{3,2,1,0:T(8,128)S(1)}, bf16[2,16,8,1024]{3,2,1,0:T(8,128)(2,1)S(1)}, f32[4,8,896]{2,1,0:T(8,128)S(1)}, f32[4,8,256]{2,1,0:T(8...) custom-call(bf16[4,2,4,4,8,768]{5,4,3,2,1,0:T(8,128)(2,1)} %bitcast.219, ...), custom_call_target="tpu_custom_call" | custom-call | bytes 62914560 | tf_op jit(solution)/shard_map/pallas_call | solution.py:594
  458.7 6.2 %collective-permute-start = (f32[8,1024]{1,0:T(8,128)S(1)}, f32[8,1024]{1,0:T(8,128)S(1)}, u32[]{:S(2)}, u32[]{:S(2)}) collective-permute-start(f32[8,1024]{1,0:T(8,128)S(1)} %bitcast.205), channel_id=1, source_target_pairs={{0,0},{1,32},{2,64},{3,96},{4,1},{5,33},{6,65},{7,97},{8,2},{9,34}... | collective-permute-start | bytes 98312 | tf_op jit(solution)/shard_map/ppermute | solution.py:1388
  472.4 1.6 copy.165
  (269 shorter events, 62.8 us)
Async XLA Ops:
  7.2 124.8 %all-gather.7.cloned.1.call-start = ((), (), s32[]{:S(2)}) async-start(), calls=%async_computation.5 | async-start | bytes 1310720 | tf_op jit(solution)/shard_map/all_gather | solution.py:1264
  14.9 4.4 copy-start
  86.0 57.9 %all-gather.5.cloned.1.call-start = ((), (), s32[]{:S(2)}) async-start(), calls=%async_computation.4 | async-start | bytes 5242880 | tf_op jit(solution)/shard_map/all_gather | solution.py:1263
  86.8 291.1 %reduce-scatter.5.cloned.1.call-start = ((), (), s32[]{:S(2)}) async-start(), calls=%async_computation.3 | async-start | bytes 1310720 | tf_op jit(solution)/shard_map/reduce_scatter | solution.py:1304
  93.9 4.5 copy-start.4
  98.4 4.7 copy-start.27
  103.1 13.7 %copy-start.10 = (bf16[1024,2048]{1,0:T(8,128)(2,1)}, bf16[1024,2048]{1,0:T(8,128)(2,1)S(1)}, u32[]{:S(2)}) copy-start(bf16[1024,2048]{1,0:T(8,128)(2,1)S(1)} %fusion.2) | copy-start | bytes 12582916
  117.7 170.8 %copy-start.54 = (f32[256]{0:T(256)}, f32[256]{0:T(256)S(1)}, u32[]{:S(2)}) copy-start(f32[256]{0:T(256)S(1)} %add_rsqrt_fusion.1) | copy-start | bytes 3076
  118.8 10.4 %copy-start.15 = (bf16[256,1024]{1,0:T(8,128)(2,1)}, bf16[256,1024]{1,0:T(8,128)(2,1)S(1)}, u32[]{:S(2)}) copy-start(bf16[256,1024]{1,0:T(8,128)(2,1)S(1)} %multiply_convert_fusion.2) | copy-start | bytes 1572868
  127.2 4.8 copy-start.64
  127.2 4.7 copy-start.65
  127.2 4.7 copy-start.66
  144.0 132.9 %copy-start.50 = (bf16[256,512]{1,0:T(8,128)(2,1)S(1)}, bf16[256,512]{1,0:T(8,128)(2,1)}, u32[]{:S(2)}) copy-start(bf16[256,512]{1,0:T(8,128)(2,1)} %get-tuple-element.107) | copy-start | bytes 786436
  144.0 134.9 %copy-start.49 = (bf16[256,512]{1,0:T(8,128)(2,1)S(1)}, bf16[256,512]{1,0:T(8,128)(2,1)}, u32[]{:S(2)}) copy-start(bf16[256,512]{1,0:T(8,128)(2,1)} %get-tuple-element.108) | copy-start | bytes 786436
  275.8 5.2 %copy-start.48 = (bf16[256,512]{1,0:T(8,128)(2,1)S(1)}, bf16[256,512]{1,0:T(8,128)(2,1)}, u32[]{:S(2)}) copy-start(bf16[256,512]{1,0:T(8,128)(2,1)} %get-tuple-element.109) | copy-start | bytes 786436
  275.8 5.2 %copy-start.51 = (bf16[2,32,2,8,384]{4,3,2,1,0:T(8,128)(2,1)S(1)}, bf16[2,32,2,8,384]{4,3,2,1,0:T(8,128)(2,1)}, u32[]{:S(2)}) copy-start(bf16[2,32,2,8,384]{4,3,2,1,0:T(8,128)(2,1)} %get-tuple-element.44) | copy-start | bytes 2359300
  317.8 7.8 %copy-start.31 = (bf16[256,512]{1,0:T(8,128)(2,1)S(1)}, bf16[256,512]{1,0:T(8,128)(2,1)}, u32[]{:S(2)}) copy-start(bf16[256,512]{1,0:T(8,128)(2,1)} %get-tuple-element.119) | copy-start | bytes 786436
  317.8 81.1 %reduce-scatter.3.cloned.1.call-start = ((), (), s32[]{:S(2)}) async-start(), calls=%async_computation.2 | async-start | bytes 5242880 | tf_op jit(solution)/shard_map/reduce_scatter | solution.py:1303
  318.9 8.3 %copy-start.28 = (bf16[1024,1024]{1,0:T(8,128)(2,1)S(1)}, bf16[1024,1024]{1,0:T(8,128)(2,1)}, u32[]{:S(2)}) copy-start(bf16[1024,1024]{1,0:T(8,128)(2,1)} %copy-done.27) | copy-start | bytes 6291460
  356.8 5.4 %copy-start.8 = (bf16[2,64,8,256]{3,2,1,0:T(8,128)(2,1)}, bf16[2,64,8,256]{3,2,1,0:T(8,128)(2,1)S(1)}, u32[]{:S(2)}) copy-start(bf16[2,64,8,256]{3,2,1,0:T(8,128)(2,1)S(1)} %get-tuple-element.52) | copy-start | bytes 1572868
  356.9 5.2 %copy-start.29 = (bf16[2,64,8,768]{3,2,1,0:T(8,128)(2,1)}, bf16[2,64,8,768]{3,2,1,0:T(8,128)(2,1)S(1)}, u32[]{:S(2)}) copy-start(bf16[2,64,8,768]{3,2,1,0:T(8,128)(2,1)S(1)} %pad_maximum_fusion) | copy-start | bytes 4718596
  359.0 5.5 %copy-start.74 = (s32[1023]{0:T(1024)S(1)}, s32[1023]{0:T(1024)}, u32[]{:S(2)}) copy-start(s32[1023]{0:T(1024)} %param.28) | copy-start | bytes 12280
  359.0 6.3 %copy-start.69 = (f32[4,8]{1,0:T(4,128)S(1)}, f32[4,8]{1,0:T(4,128)}, u32[]{:S(2)}) copy-start(f32[4,8]{1,0:T(4,128)} %fusion.121) | copy-start | bytes 388
  366.1 7.4 %copy-start.26 = (bf16[2,4,16,8,1024]{4,3,2,1,0:T(8,128)(2,1)S(1)}, bf16[2,4,16,8,1024]{4,3,2,1,0:T(8,128)(2,1)}, u32[]{:S(2)}) copy-start(bf16[2,4,16,8,1024]{4,3,2,1,0:T(8,128)(2,1)} %multiply_convert_fusion) | copy-start | bytes 6291460
  456.7 8.9 %copy-start.39 = (bf16[256,512]{1,0:T(8,128)(2,1)S(1)}, bf16[256,512]{1,0:T(8,128)(2,1)}, u32[]{:S(2)}) copy-start(bf16[256,512]{1,0:T(8,128)(2,1)} %get-tuple-element.105) | copy-start | bytes 786436
  456.7 8.9 %copy-start.47 = (bf16[256,512]{1,0:T(8,128)(2,1)S(1)}, bf16[256,512]{1,0:T(8,128)(2,1)}, u32[]{:S(2)}) copy-start(bf16[256,512]{1,0:T(8,128)(2,1)} %get-tuple-element.117) | copy-start | bytes 786436
  456.7 9.2 %copy-start.38 = (bf16[256,512]{1,0:T(8,128)(2,1)S(1)}, bf16[256,512]{1,0:T(8,128)(2,1)}, u32[]{:S(2)}) copy-start(bf16[256,512]{1,0:T(8,128)(2,1)} %get-tuple-element.104) | copy-start | bytes 786436
  456.7 9.2 %copy-start.46 = (bf16[256,512]{1,0:T(8,128)(2,1)S(1)}, bf16[256,512]{1,0:T(8,128)(2,1)}, u32[]{:S(2)}) copy-start(bf16[256,512]{1,0:T(8,128)(2,1)} %get-tuple-element.120) | copy-start | bytes 786436
  457.4 13.7 %copy-start.53 = (f32[8,128]{1,0:T(8,128)}, f32[8,128]{1,0:T(8,128)S(1)}, u32[]{:S(2)}) copy-start(f32[8,128]{1,0:T(8,128)S(1)} %slice_reduce_fusion.2) | copy-start | bytes 12292
  457.4 8.9 %copy-start.37 = (bf16[256,512]{1,0:T(8,128)(2,1)S(1)}, bf16[256,512]{1,0:T(8,128)(2,1)}, u32[]{:S(2)}) copy-start(bf16[256,512]{1,0:T(8,128)(2,1)} %get-tuple-element.103) | copy-start | bytes 786436
  457.4 8.9 %copy-start.45 = (bf16[256,512]{1,0:T(8,128)(2,1)S(1)}, bf16[256,512]{1,0:T(8,128)(2,1)}, u32[]{:S(2)}) copy-start(bf16[256,512]{1,0:T(8,128)(2,1)} %get-tuple-element.121) | copy-start | bytes 786436
  458.7 13.1 %collective-permute-start = (f32[8,1024]{1,0:T(8,128)S(1)}, f32[8,1024]{1,0:T(8,128)S(1)}, u32[]{:S(2)}, u32[]{:S(2)}) collective-permute-start(f32[8,1024]{1,0:T(8,128)S(1)} %bitcast.205), channel_id=1, source_target_pairs={{0,0},{1,32},{2,64},{3,96},{4,1},{5,33},{6,65},{7,97},{8,2},{9,34}... | collective-permute-start | bytes 98312 | tf_op jit(solution)/shard_map/ppermute | solution.py:1388
  (48 other events, 108.2 us)
Sparse Core Ops, SparseCore 0:
  86.1 17.5 all-gather.6
  105.9 37.9 all-gather.4
  317.9 27.2 reduce-scatter.4
  347.9 50.9 reduce-scatter.2

commit v2 on v1

--- a/solution.py
+++ b/solution.py
@@ -29,6 +29,7 @@
 PARTS = ((0, 1536), (1536, 1408), (2944, 1408))
 ORDERS = ("xyz", "yzx", "zxy")
 TAIL = 256 + 128
+PACK = 1024 + 256
 GRAD = 3 * 256 + 128 + 256
 THIRD = GRAD // 3
 
@@ -208,12 +209,10 @@
 def gather_kernel(
     slab,
     own,
-    main,
-    extra,
+    slabs,
     full,
     items,
-    mains,
-    extras,
+    arrived_slabs,
     relay,
     local,
     send,
@@ -236,7 +235,7 @@
         return device(spot["x"], spot["y"], spot["z"], core)
 
     greet_peers([who(moved(axis, by)) for axis in "xyz" for by in (1, 3)] + [sibling])
-    packets = Exchange((main, extra), (mains, extras), *exchange_sems)
+    packets = Exchange((slabs,), (arrived_slabs,), *exchange_sems)
 
     def block(spot, whole, first, width):
         every = slice(None)
@@ -315,17 +314,16 @@
         copy.wait_send()
 
 
-def gather_all(slab, own, main, extra):
+def gather_all(slab, own, slabs):
     return pl.pallas_call(
         gather_kernel,
         out_shape=(
             jax.ShapeDtypeStruct((4, 2, 4, 2, 2, 8, SLAB), BF16),
             jax.ShapeDtypeStruct((2, 4, 16, 8, D), BF16),
-            jax.ShapeDtypeStruct((32, 2, 8, D), BF16),
-            jax.ShapeDtypeStruct((32, 2, 8, 256), BF16),
+            jax.ShapeDtypeStruct((32, 2, 8, PACK), BF16),
         ),
-        in_specs=[ANY] * 4,
-        out_specs=(ANY,) * 4,
+        in_specs=[ANY] * 3,
+        out_specs=(ANY,) * 3,
         scratch_shapes=[
             pltpu.VMEM((2, 16, 8, D), BF16),
             DMA(()),
@@ -340,7 +338,7 @@
         ],
         compiler_params=params(0, 32),
         cost_estimate=cost(90 << 20),
-    )(slab, own, main, extra)
+    )(slab, own, slabs)
 
 
 def items_kernel(own, full, relay, local, send, recv):
@@ -373,14 +371,12 @@
     heads,
     rest,
     part,
-    main,
-    extra,
+    outs,
     mine,
     other,
     small,
     wide,
-    mains,
-    extras,
+    arrived_outs,
     own,
     got,
     relay,
@@ -466,7 +462,7 @@
                 )
                 firsts.append((index, copy))
             copy.start()
-    packets = Exchange((main, extra), (mains, extras), *exchange_sems)
+    packets = Exchange((outs,), (arrived_outs,), *exchange_sems)
     packets.start(1, 32)
     packets.keep()
 
@@ -589,7 +585,7 @@
             second(index, k).wait_send()
 
 
-def reduce_grads(heads, rest, part, main, extra):
+def reduce_grads(heads, rest, part, outs):
     columns = 3 * 256 + 128
     return pl.pallas_call(
         grads_kernel,
@@ -598,11 +594,10 @@
             jax.ShapeDtypeStruct((2, 16, 8, D), BF16),
             jax.ShapeDtypeStruct((4, 8, columns), F32),
             jax.ShapeDtypeStruct((4, 8, 256), F32),
-            jax.ShapeDtypeStruct((32, 2, 8, D), BF16),
-            jax.ShapeDtypeStruct((32, 2, 8, 256), BF16),
+            jax.ShapeDtypeStruct((32, 2, 8, PACK), BF16),
         ),
-        in_specs=[ANY] * 5,
-        out_specs=(VMEM, ANY, VMEM, VMEM, ANY, ANY),
+        in_specs=[ANY] * 4,
+        out_specs=(VMEM, ANY, VMEM, VMEM, ANY),
         scratch_shapes=[
             pltpu.VMEM((2, 2, 16, 8, D), BF16),
             pltpu.VMEM((2, 2, 16, 8, D), BF16),
@@ -636,7 +631,7 @@
         ],
         compiler_params=params(4, 48),
         cost_estimate=cost(60 << 20),
-    )(heads, rest, part, main, extra)
+    )(heads, rest, part, outs)
 
 
 NT = (((1,), (1,)), ((), ()))
@@ -812,15 +807,13 @@
 def moe_kernel(
     main,
     tail,
-    grads_main,
-    grads_extra,
+    grads,
     gate_w,
     up_w,
     down_w,
     back_main,
     back_tail,
-    out_main,
-    out_extra,
+    outs,
     dgate,
     dup,
     ddown,
@@ -828,10 +821,8 @@
     own_tail,
     sib_main,
     sib_tail,
-    grad_main,
-    grad_extra,
-    res_main,
-    res_extra,
+    grad_held,
+    res_held,
     part_main,
     part_tail,
     give_main,
@@ -897,13 +888,12 @@
         copies = []
         for side in range(2):
             dp, seq = device(*chips(block * per + j)[1], core if side == 0 else 1 - core)
-            for i, (source, held) in enumerate(((grads_main, grad_main), (grads_extra, grad_extra))):
-                place_at = side * per + j
-                copies.append(
-                    pltpu.make_async_copy(
-                        source.at[seq, dp], held.at[slot, place_at], grad_sem.at[i, slot, place_at]
-                    )
+            spot = side * per + j
+            copies.append(
+                pltpu.make_async_copy(
+                    grads.at[seq, dp], grad_held.at[slot, spot], grad_sem.at[slot, spot]
                 )
+            )
         return copies
 
     def results(block, j):
@@ -911,13 +901,12 @@
         copies = []
         for side in range(2):
             dp, seq = device(*chips(block * per + j)[1], core if side == 0 else 1 - core)
-            for i, (held, target) in enumerate(((res_main, out_main), (res_extra, out_extra))):
-                place_at = side * per + j
-                copies.append(
-                    pltpu.make_async_copy(
-                        held.at[slot, place_at], target.at[seq, dp], res_sem.at[i, slot, place_at]
-                    )
+            spot = side * per + j
+            copies.append(
+                pltpu.make_async_copy(
+                    res_held.at[slot, spot], outs.at[seq, dp], res_sem.at[slot, spot]
                 )
+            )
         return copies
 
     def each(copies, block, act):
@@ -996,9 +985,8 @@
         rows = jnp.concatenate(
             [rows_of(own_main[some]), rows_of(sib_main[some]), whole(tails[:, :256])], 0
         )
-        grads = jnp.concatenate(
-            [rows_of(grad_main[slot]), whole(rows_of(grad_extra[slot]))], 0
-        )
+        held = rows_of(grad_held[slot])
+        row_grads = jnp.concatenate([held[:, :D], whole(held[:, D:])], 0)
         scalars = jnp.concatenate([tails[:, 256:].astype(F32), dot(picks[0], tails[:, 256:])], 0)
         first = lax.broadcasted_iota(jnp.int32, (320, 1), 0) < 256
         gates = jnp.where(
@@ -1007,10 +995,11 @@
             scalars[:, 2:3] + scalars[:, 3:4],
         )
         out, grad_rows, grad_gates = expert_rows(
-            rows, grads, gates, gate_w, up_w, down_w, dgate, dup, ddown
+            rows, row_grads, gates, gate_w, up_w, down_w, dgate, dup, ddown
         )
-        res_main[slot] = packets_of(out[:256])
-        res_extra[slot] = packets_of(quarters(out[256:]))
+        res_held[slot] = packets_of(
+            jnp.concatenate([out[:256], quarters(out[256:]).astype(BF16)], 1)
+        )
         lane = lax.broadcasted_iota(jnp.int32, (320, 128), 1)
         lanes = jnp.where(lane == jnp.where(first, 0, 1), grad_gates, 0.0)
         extra_lanes = lanes[256:].astype(BF16)
@@ -1096,27 +1085,26 @@
         copy.wait()
 
 
-def run_experts(main, tail, grads_main, grads_extra, gate_w, up_w, down_w):
+def run_experts(main, tail, grads, gate_w, up_w, down_w):
     wide = gate_w.shape[0]
     grad = jax.ShapeDtypeStruct((wide, D), F32)
 
     def pair(count):
         return [pltpu.VMEM((count, 2, 8, D), BF16), pltpu.VMEM((count, 2, 8, TAIL), BF16)]
 
-    staged = [pltpu.VMEM((2, 16, 2, 8, D), BF16), pltpu.VMEM((2, 16, 2, 8, 256), BF16)]
+    staged = [pltpu.VMEM((2, 16, 2, 8, PACK), BF16)]
     return pl.pallas_call(
         moe_kernel,
         out_shape=(
             jax.ShapeDtypeStruct((2, 32, 2, 8, D), BF16),
             jax.ShapeDtypeStruct((2, 32, 2, 8, TAIL), BF16),
-            jax.ShapeDtypeStruct((4, 32, 2, 8, D), BF16),
-            jax.ShapeDtypeStruct((4, 32, 2, 8, 256), BF16),
+            jax.ShapeDtypeStruct((4, 32, 2, 8, PACK), BF16),
             grad,
             grad,
             grad,
         ),
-        in_specs=[ANY] * 4 + [VMEM] * 3,
-        out_specs=(ANY,) * 4 + (VMEM,) * 3,
+        in_specs=[ANY] * 3 + [VMEM] * 3,
+        out_specs=(ANY,) * 3 + (VMEM,) * 3,
         scratch_shapes=pair(64)
         + pair(64)
         + staged
@@ -1126,13 +1114,13 @@
         + pair(64)
         + [DMA((2,))]
         + [DMA((2, 64))] * 4
-        + [DMA((2, 2, 16))] * 2
+        + [DMA((2, 16))] * 2
         + [DMA((2, 8))] * 2
         + [DMA((2,))]
         + [DMA((2, 64))] * 2,
         compiler_params=params(2, 60),
         cost_estimate=cost(90 << 20, 33 << 30),
-    )(main, tail, grads_main, grads_extra, gate_w, up_w, down_w)
+    )(main, tail, grads, gate_w, up_w, down_w)
 
 
 def rms_forward(values, gain):
@@ -1186,18 +1174,14 @@
     extra_place = jnp.where(
         (slots >= MAIN) & (slots < CAP), route_flat * 4 + slots - MAIN, -1
     )
-    hot_extra = extra_place[:, :, None] == (columns // 4)[None, None, :]
-    quarter = jnp.arange(4, dtype=jnp.int32)
-    quarter_hot = quarter[:, None] == (columns % 4)[None, :]
-
-    def spread(values_k):
-        hot_m = hot_main.astype(BF16)
-        hot_x = (hot_extra[None] & quarter_hot[:, None, None, :]).astype(BF16)
-        main = jnp.einsum("tkc,td->cd", hot_m, values_k, preferred_element_type=F32)
-        extra = jnp.einsum(
-            "mtkc,tmd->cd", hot_x, values_k.reshape(tokens, 4, 256), preferred_element_type=F32
-        )
-        return main.astype(BF16), extra.astype(BF16)
+    hot_extra = extra_place[:, :, None] == columns[None, None, : EXPERTS * 4]
+    hot_main_both = jnp.sum(hot_main.astype(BF16), 1)
+    hot_extra_both = jnp.sum(hot_extra.astype(BF16), 1)
+
+    def spread(values):
+        main = dot(hot_main_both, values, TN).astype(BF16)
+        extra = dot(hot_extra_both, values, TN).astype(BF16)
+        return main, extra.reshape(EXPERTS * MAIN, 256)
 
     slab = jnp.concatenate(
         [
@@ -1215,11 +1199,10 @@
         1,
     )
     grad_main, grad_extra = spread(cotangent.reshape(tokens, D))
-    full, items, grads_main, grads_extra = gather_all(
+    full, items, route_grads = gather_all(
         slab,
         layer_in.reshape(2, 16, 8, D),
-        grad_main.reshape(EXPERTS, 2, 8, D),
-        grad_extra.reshape(EXPERTS, 2, 8, 256),
+        jnp.concatenate([grad_main, grad_extra], 1).reshape(EXPERTS, 2, 8, PACK),
     )
 
     full = full.reshape(D, SLAB)
@@ -1258,35 +1241,30 @@
     rows_main, rows_extra = spread(hidden_two)
     gate_main = jnp.sum(jnp.where(hot_main, gates[:, :, None], 0.0), (0, 1))
     gate_extra = jnp.sum(jnp.where(hot_extra, gates[:, :, None], 0.0), (0, 1))
+    gate_extra = jnp.repeat(gate_extra, 4)
     lanes = jnp.stack(split(gate_main) + split(gate_extra), -1)
     rows_tail = jnp.concatenate([rows_extra, jnp.pad(lanes, ((0, 0), (0, 124)))], -1)
-    grads_main = lax.all_gather(grads_main, "seq", axis=0, tiled=False)
-    grads_extra = lax.all_gather(grads_extra, "seq", axis=0, tiled=False)
-    returned, returned_tail, out_main, out_extra, *expert_grads = run_experts(
+    route_grads = lax.all_gather(route_grads, "seq", axis=0, tiled=False)
+    returned, returned_tail, outs, *expert_grads = run_experts(
         rows_main.reshape(EXPERTS, 2, 8, D),
         rows_tail.reshape(EXPERTS, 2, 8, TAIL),
-        grads_main,
-        grads_extra,
+        route_grads,
         expert_gate[0].T,
         expert_up[0].T,
         expert_down[0],
     )
     grad_gate, grad_up, grad_down = expert_grads[0].T, expert_grads[1].T, expert_grads[2]
 
-    hot_both = jnp.sum(hot_main.astype(BF16), 1)
-    hot_extra_both = jnp.sum(hot_extra.astype(BF16), 1)
-    quarters = [hot_extra_both * quarter_hot[m][None, :].astype(BF16) for m in range(4)]
-    back = returned.reshape(2 * EXPERTS * MAIN, D)
     back_tail = returned_tail.reshape(2 * EXPERTS * MAIN, TAIL)
-    from_main = dot(jnp.concatenate([hot_both, hot_both], 1), back)
-    from_extra = jnp.concatenate(
-        [dot(jnp.concatenate([hot, hot], 1), back_tail[:, :256]) for hot in quarters], 1
-    )
-    grad_from_experts = from_main + from_extra
+    back_extra = back_tail[:, :256].reshape(2 * EXPERTS * 4, D)
+    grad_from_experts = dot(
+        jnp.concatenate([hot_main_both, hot_main_both], 1), returned.reshape(2 * EXPERTS * MAIN, D)
+    ) + dot(jnp.concatenate([hot_extra_both, hot_extra_both], 1), back_extra)
     returned_gates = back_tail[:, 256:258].astype(F32).reshape(2, EXPERTS * MAIN, 2)
     returned_gates = returned_gates[0] + returned_gates[1]
-    grad_gates = jnp.sum(jnp.where(hot_main, returned_gates[:, 0], 0.0), -1) + 0.25 * jnp.sum(
-        jnp.where(hot_extra, returned_gates[:, 1], 0.0), -1
+    extra_gates = returned_gates[:, 1].reshape(EXPERTS * 4, 4)[:, 0]
+    grad_gates = jnp.sum(jnp.where(hot_main, returned_gates[:, 0], 0.0), -1) + jnp.sum(
+        jnp.where(hot_extra, extra_gates, 0.0), -1
     )
 
     grad_final = cotangent.astype(F32).reshape(tokens, D)
@@ -1297,11 +1275,8 @@
     grad_gain_moe = jnp.sum(grad_hidden_two * normed_two, 0)
     grad_resid = grad_final + rms_values(grad_hidden_two, normed_two, factor_two, gain_moe)
     grad_attended = gather_items(grad_resid.astype(BF16).reshape(2, 16, 8, D))
-    grad_attended, out_main, out_extra = lax.optimization_barrier(
-        (grad_attended, out_main, out_extra)
-    )
-    out_main = lax.psum_scatter(out_main, "seq", scatter_dimension=0, tiled=False)
-    out_extra = lax.psum_scatter(out_extra, "seq", scatter_dimension=0, tiled=False)
+    grad_attended, outs = lax.optimization_barrier((grad_attended, outs))
+    outs = lax.psum_scatter(outs, "seq", scatter_dimension=0, tiled=False)
     grad_attended = grad_attended.reshape(4 * tokens, D)
 
     first = seq * 256
@@ -1354,29 +1329,22 @@
         -1,
     ).astype(BF16)
     rest = jnp.concatenate([smalls_grad, grad_out], -1)
-    mine, other, small_sums, wide_sums, out_main, out_extra = reduce_grads(
+    mine, other, small_sums, wide_sums, outs = reduce_grads(
         grad_qkv.reshape(4, 2, 4, 4, 8, 768),
         rest.reshape(4, 2, 4, 4, 8, 384),
         part_hidden.astype(BF16).reshape(2, 4, 16, 8, D),
-        out_main,
-        out_extra,
+        outs,
     )
 
     gated_main = split(jnp.sum(jnp.where(hot_main, gates[:, :, None], 0.0), 1))
     gated_extra = split(jnp.sum(jnp.where(hot_extra, gates[:, :, None], 0.0), 1))
-    out_main = out_main.reshape(EXPERTS * MAIN, D)
-    out_extra = out_extra.reshape(EXPERTS * MAIN, 256)
-    moe_out = dot(
-        jnp.concatenate(gated_main, 1), jnp.concatenate([out_main, out_main], 0)
-    ) + jnp.concatenate(
-        [
-            dot(
-                jnp.concatenate([part * quarter_hot[m][None, :].astype(BF16) for part in gated_extra], 1),
-                jnp.concatenate([out_extra, out_extra], 0),
-            )
-            for m in range(4)
-        ],
-        1,
+    outs = outs.reshape(EXPERTS * MAIN, PACK)
+    out_main, out_extra = outs[:, :D], outs[:, D:].reshape(EXPERTS * 4, D)
+    moe_out = (
+        dot(gated_main[0], out_main)
+        + dot(gated_main[1], out_main)
+        + dot(gated_extra[0], out_extra)
+        + dot(gated_extra[1], out_extra)
     )
     layer_out = (resid + moe_out).astype(BF16).reshape(2, ROWS, D)
 

time: 491 us -> 467 us (0.951)
  waiting for transfers between devices: 34.3 us -> 0.04 us
  local copies, waits for them, and re-layouts: 48.5 us -> 58.1 us
  Pallas kernels: 311 us -> 306 us
    reduce_scatter x2 -> x1, waiting for transfers between devices: 21 us -> 0.01 us  [body(): outs = lax.psum_scatter(outs, 'seq', scatter_dimension=0, tiled=False)]
    all_gather x2 -> x1, waiting for transfers between devices: 12 us -> 0.01 us  [body(): route_grads = lax.all_gather(route_grads, 'seq', axis=0, tiled=False)]
    pallas_call x1, Pallas kernels: 132 us -> 124 us  [run_experts(): pl.pallas_call(moe_kernel, out_shape=(jax.ShapeDtypeStruct((2, 32, 2, 8,...]
    dot_general x4 -> x0, matrix products: 6.25 us -> none  [the longest x2 3.96 us: spread(): main = jnp.einsum('tkc,td->cd', hot_m, values_k, preferred_element_type=F32)]
    pallas_call x1, Pallas kernels: 27 us -> 32.3 us  [gather_items(): pl.pallas_call(items_kernel, out_shape=jax.ShapeDtypeStruct((2, 4, 16, 8,...]
    unnamed x156 -> x137, local copies, waits for them, and re-layouts: 25.1 us -> 28.2 us
    dot_general x6 -> x10, matrix products: 15.8 us -> 18.8 us  [dot(): return lax.dot_general(a, b, dims, preferred_element_type=F32)]
    dot_general x15 -> x11, matrix products: 23.2 us -> 25.7 us  [dot(): return jnp.dot(a, b, preferred_element_type=F32)]
  transfers between devices with their start and end apart: 5 -> 3, of which waited for: 2 -> 0; matrix products, arithmetic and copies ran while one was open for 14% -> 17% of each run, Pallas kernels for 7% -> 8%
where the time goes in v2:
time: 467 us; the launch traced here: 461 us
  Pallas kernels  306 us (66%)
  local copies, waits for them, and re-layouts  58.1 us (12%)
  matrix products  45.6 us (10%)
  other arithmetic  29.7 us (6%)
  between operations  15.4 us (3%)
  starting transfers between devices  6.13 us (1%)
    pallas_call x1, Pallas kernels, run_experts(): pl.pallas_call(moe_kernel, out_shape=(jax.ShapeDtypeStruct((2, 32, 2, 8,...  124 us
    pallas_call x1, Pallas kernels, gather_all(): pl.pallas_call(gather_kernel, out_shape=(jax.ShapeDtypeStruct((4, 2, 4, 2...  60.8 us
    pallas_call x1, Pallas kernels, reduce_grads(): pl.pallas_call(grads_kernel, out_shape=(jax.ShapeDtypeStruct((2, 16, 8, D...  53.5 us
    pallas_call x1, Pallas kernels, gather_items(): pl.pallas_call(items_kernel, out_shape=jax.ShapeDtypeStruct((2, 4, 16, 8,...  32.3 us
    unnamed x137, local copies, waits for them, and re-layouts  28.2 us
    dot_general x11, matrix products, dot(): return jnp.dot(a, b, preferred_element_type=F32)  25.7 us
    pallas_call x1, Pallas kernels, attend_back(): pl.pallas_call(backward_kernel, grid=(2, 2), out_shape=(shape,) * 4 + (ja...  21.6 us
    dot_general x10, matrix products, dot(): return lax.dot_general(a, b, dims, preferred_element_type=F32)  18.8 us
  transfers between devices with their start and end apart: 3, of which 0 were waited for; matrix products, arithmetic and copies ran while one was open for 17% of the time, Pallas kernels for 8%

profile of v2, /device:TPU:5, one launch (start us, length us, event | category | flops | bytes accessed | tf_op | source)
XLA Modules:
  0.0 460.9 jit_solution(8094156403447243543)
XLA Ops:
  17.8 60.8 %shard_map.254 = (bf16[4,2,4,2,2,8,4352]{6,5,4,3,2,1,0:T(8,128)(2,1)S(1)}, bf16[2,4,16,8,1024]{4,3,2,1,0:T(8,128)(2,1)S(1)}, bf16[32,2,8,1280]{3,2,1,0:T(8,128)(2,1)S(1)}) custom-call(bf16[8,4352]{1,0:T(8,128)(2,1)S(1)} %concatenate.48.slab, bf16[2,16,8,1024]{3,2,1,0:T(8,128)(2,1)S(1)} %bitcast.167, bf16[32,2,8,1280]{3,2,1,0:T(8,128)(2,1)S(1)} %copy-done.2), custom_call_target="tpu_custom_call" | custom-call | bytes 94371840 | tf_op jit(solution)/shard_map/pallas_call | solution.py:318
  79.7 3.4 copy-done.5
  83.8 2.7 constant_dynamic-slice_fusion.1
  93.1 2.6 fusion.21
  96.3 7.7 %fusion.2 = bf16[1024,2048]{1,0:T(8,128)(2,1)S(1)} fusion(bf16[1024,1024]{1,0:T(8,128)(2,1)S(1)} %multiply_convert_fusion.1, bf16[1024,4352]{1,0:T(8,128)(2,1)} %bitcast.179), kind=kOutput, calls=%fused_computation.7 | convolution fusion | flops 4297064448 | bytes 10485760 | tf_op jit(solution)/shard_map/dot_general | solution.py:643
  104.0 13.7 %shard_map.255 = bf16[2,16,8,1024]{3,2,1,0:T(8,128)(2,1)S(1)} custom-call(f32[8,2,640]{2,1,0:T(2,128)S(1)} %reshape.462.window, bf16[2,16,8,1024]{3,2,1,0:T(8,128)(2,1)S(1)} %bitcast.192, bf16[2,64,8,2048]{3,2,1,0:T(8,128)(2,1)S(1)} %bitcast.187, bf16[2,64,8,2048]{3,2,1,0:T(8,128)(2,1)S(1)} %bitcast.188), custom_call_target="tpu_custom_call" | custom-call | flops 4294967296 | bytes 12582912 | tf_op jit(solution)/shard_map/pallas_call | solution.py:685
  117.8 2.4 multiply_reduce_fusion.4
  129.9 1.8 concatenate.53
  131.7 1.7 select_reduce_fusion.1
  137.3 1.7 pad_maximum_fusion.2.tail
  140.5 124.1 %shard_map.256 = (bf16[2,32,2,8,1024]{4,3,2,1,0:T(8,128)(2,1)}, bf16[2,32,2,8,384]{4,3,2,1,0:T(8,128)(2,1)}, bf16[4,32,2,8,1280]{4,3,2,1,0:T(8,128)(2,1)}, f32[7...) custom-call(bf16[32,2,8,1024]{3,2,1,0:T(8,128)(2,1)} %bitcast.207, ...), custom_call_target="tpu_custom_call" | custom-call | flops 35433480192 | bytes 94371840 | tf_op jit(solution)/shard_map/pallas_call | solution.py:1096
  264.6 1.7 slice.151
  266.2 1.9 slice.150
  268.1 3.3 fusion.34
  272.4 2.2 reshape.475
  279.6 2.6 multiply_reduce_fusion.2
  283.2 32.3 %shard_map.257 = bf16[2,4,16,8,1024]{4,3,2,1,0:T(8,128)(2,1)S(1)} custom-call(bf16[2,16,8,1024]{3,2,1,0:T(8,128)(2,1)S(1)} %bitcast.174), custom_call_target="tpu_custom_call" | custom-call | bytes 20971520 | tf_op jit(solution)/shard_map/pallas_call | solution.py:359
  320.7 2.3 constant_dynamic-slice_fusion.2
  323.0 2.7 convolution_convert_fusion.5
  325.7 1.9 multiply_convert_fusion
  329.1 2.7 convolution_convert_fusion.4
  331.8 21.6 %shard_map.258 = (bf16[2,64,8,256]{3,2,1,0:T(8,128)(2,1)S(1)}, bf16[2,64,8,256]{3,2,1,0:T(8,128)(2,1)S(1)}, bf16[2,64,8,256]{3,2,1,0:T(8,128)(2,1)S(1)}, bf16[2,...) custom-call(f32[2,2,4,640]{3,2,1,0:T(4,128)S(1)} %pad_maximum_fusion.3.windows, bf16[2,64,8,256]{3,2,1,0:T(8,128)(2,1)S(1)} %bitcast.190, ...), custom_call_target="tpu_custom_call" | custom-call | flops 8589934592 | bytes 12582912 | tf_op jit(solution)/shard_map/pallas_call | solution.py:756
  356.0 1.6 pad_maximum_fusion
  357.9 3.2 fusion.77
  362.4 2.3 convolution_convert_fusion.3
  364.8 3.0 concatenate.63.rest
  367.8 5.0 %convolution_convert_fusion = bf16[1024,768]{1,0:T(8,128)(2,1)} fusion(bf16[1024,1024]{1,0:T(8,128)(2,1)} %bitcast.200, bf16[1024,768]{1,0:T(8,128)(2,1)} %bitcast.204), kind=kOutput, calls=%fused_computation.12 | convolution fusion | flops 1611399168 | bytes 5242880 | tf_op jit(solution)/shard_map/dot_general | solution.py:644
  374.2 53.5 %shard_map.259 = (f32[2,16,8,1024]{3,2,1,0:T(8,128)S(1)}, bf16[2,16,8,1024]{3,2,1,0:T(8,128)(2,1)S(1)}, f32[4,8,896]{2,1,0:T(8,128)S(1)}, f32[4,8,256]{2,1,0:T(8,128)S(1)}, bf16[32,2,8,1280]{3,2,1,0:T(8,128)(2,1)S(1)}) custom-call(bf16[4,2,4,4,8,768]{5,4,3,2,1,0:T(8,128)(2,1)} %bitcast.205, bf16[4,2,4,4,8,384]{5,4,3,2,1,0:T(8,128)(2,1)S(1)} %concatenate.63.rest, ...), custom_call_target="tpu_custom_call" | custom-call | bytes 62914560 | tf_op jit(solution)/shard_map/pallas_call | solution.py:590
  429.9 6.1 %collective-permute-start = (f32[8,1024]{1,0:T(8,128)S(1)}, f32[8,1024]{1,0:T(8,128)S(1)}, u32[]{:S(2)}, u32[]{:S(2)}) collective-permute-start(f32[8,1024]{1,0:T(8,128)S(1)} %bitcast.189), channel_id=1, source_target_pairs={{0,0},{1,32},{2,64},{3,96},{4,1},{5,33},{6,65},{7,97},{8,2},{9,34}... | collective-permute-start | bytes 98312 | tf_op jit(solution)/shard_map/ppermute | solution.py:1356
  442.0 3.0 fusion.28
  446.4 1.6 copy.98
  449.2 1.6 copy.99
  (242 shorter events, 66.8 us)
Async XLA Ops:
  7.2 7.4 %copy-start.20 = (bf16[2,128,1024]{2,1,0:T(8,128)(2,1)S(1)}, bf16[2,128,1024]{2,1,0:T(8,128)(2,1)}, u32[]{:S(2)}) copy-start(bf16[2,128,1024]{2,1,0:T(8,128)(2,1)} %param.29) | copy-start | bytes 1572868
  7.2 8.0 %copy-start.62 = (bf16[4]{0:T(256)(128)(2,1)S(1)}, bf16[4]{0:T(256)(128)(2,1)}, u32[]{:S(2)}) copy-start(bf16[4]{0:T(256)(128)(2,1)} %param.22) | copy-start | bytes 28
  7.2 133.3 %all-gather.3.cloned.1.call-start = ((), (), s32[]{:S(2)}) async-start(), calls=%async_computation.2 | async-start | bytes 6553600 | tf_op jit(solution)/shard_map/all_gather | solution.py:1247
  79.7 3.4 copy-start.5
  83.1 289.7 %reduce-scatter.2.cloned.1.call-start = ((), (), s32[]{:S(2)}) async-start(), calls=%async_computation.1 | async-start | bytes 6553600 | tf_op jit(solution)/shard_map/reduce_scatter | solution.py:1279
  83.8 12.0 %copy-start.51 = (f32[1024]{0:T(1024)}, f32[1024]{0:T(1024)S(1)}, u32[]{:S(2)}) copy-start(f32[1024]{0:T(1024)S(1)} %rsqrt.39) | copy-start | bytes 12292
  83.8 4.5 copy-start.63
  92.9 2.8 copy-start.53
  96.3 7.7 %copy-start.26 = (bf16[1024,1024]{1,0:T(8,128)(2,1)}, bf16[1024,1024]{1,0:T(8,128)(2,1)S(1)}, u32[]{:S(2)}) copy-start(bf16[1024,1024]{1,0:T(8,128)(2,1)S(1)} %multiply_convert_fusion.1) | copy-start | bytes 6291460
  104.0 13.7 %copy-start.13 = (bf16[1024,2048]{1,0:T(8,128)(2,1)}, bf16[1024,2048]{1,0:T(8,128)(2,1)S(1)}, u32[]{:S(2)}) copy-start(bf16[1024,2048]{1,0:T(8,128)(2,1)S(1)} %fusion.2) | copy-start | bytes 12582916
  120.2 2.4 copy-start.38
  120.2 2.3 copy-start.42
  123.8 2.8 copy-start.50
  271.4 8.2 %copy-start.43 = (f32[256]{0:T(256)S(1)}, f32[256]{0:T(256)}, u32[]{:S(2)}) copy-start(f32[256]{0:T(256)} %copy-done.42) | copy-start | bytes 3076
  275.7 3.8 copy-start.16
  279.6 2.6 copy-start.21
  282.2 33.3 %copy-start.55 = (f32[256]{0:T(256)}, f32[256]{0:T(256)S(1)}, u32[]{:S(2)}) copy-start(f32[256]{0:T(256)S(1)} %broadcast_multiply_fusion.1) | copy-start | bytes 3076
  316.8 3.1 copy-start.36
  320.1 2.9 copy-start.27
  329.1 2.7 copy-start.8
  329.1 2.7 copy-start.9
  329.1 2.7 copy-start.14
  357.6 3.4 copy-start.28
  357.9 3.6 copy-start.64
  357.9 4.4 copy-start.58
  361.1 3.7 copy-start.30
  428.6 9.0 %copy-start.22 = (f32[256,512]{1,0:T(8,128)S(1)}, f32[256,512]{1,0:T(8,128)}, u32[]{:S(2)}) copy-start(f32[256,512]{1,0:T(8,128)} %get-tuple-element.64) | copy-start | bytes 1572868
  428.7 16.4 %copy-start.39 = (f32[8,128]{1,0:T(8,128)}, f32[8,128]{1,0:T(8,128)S(1)}, u32[]{:S(2)}) copy-start(f32[8,128]{1,0:T(8,128)S(1)} %slice_reduce_fusion.3) | copy-start | bytes 12292
  429.9 15.9 %collective-permute-start = (f32[8,1024]{1,0:T(8,128)S(1)}, f32[8,1024]{1,0:T(8,128)S(1)}, u32[]{:S(2)}, u32[]{:S(2)}) collective-permute-start(f32[8,1024]{1,0:T(8,128)S(1)} %bitcast.189), channel_id=1, source_target_pairs={{0,0},{1,32},{2,64},{3,96},{4,1},{5,33},{6,65},{7,97},{8,2},{9,34}... | collective-permute-start | bytes 98312 | tf_op jit(solution)/shard_map/ppermute | solution.py:1356
  442.0 4.4 copy-start.25
  446.4 2.9 copy-start.24
  449.2 2.9 copy-start.23
  (36 other events, 47.4 us)
Sparse Core Ops, SparseCore 0:
  83.2 40.7 all-gather.2
  316.9 53.9 reduce-scatter.1
